TPU v7x, 512 devices: a whole 4x8x8 slice. The times are simulated.
512 devices in a mesh: replica: 32 (over z, y_hi), tensor: 16 (over y_lo, x, core).
Axes of the slice: x: 4, y: 8 (y_hi: 4, y_lo: 2; y = y_hi * 2 + y_lo), z: 8, core: 2. Of those that a mesh axis runs over, the one named last changes fastest.
Arguments:
- pseudo_grad: bfloat16 [32, 8192, 512], P('replica', 'tensor'), may hold values from -0.1796875 to 0.1796875
- stale_avg: bfloat16 [8192, 512], P('tensor'), may hold values from -0.011962891 to 0.011962891
- momentum: float32 [16, 32, 16, 512], P('tensor', 'replica'), may hold values from -0.012 to 0.012
- weight: bfloat16 [8192, 512], P('tensor'), may hold values from -0.0625 to 0.0625
- tokens: bfloat16 [32768, 8192], P('replica', 'tensor'), may hold values from -6 to 6
- cotangent: bfloat16 [32768, 512], P(('replica', 'tensor')), may hold values from -6 to 6
Outputs:
- avg_codes: float32 [16, 32, 16, 512], P('tensor', 'replica')
- avg_scales: float32 [16, 32, 16, 4], P('tensor', 'replica')
- new_momentum: float32 [16, 32, 16, 512], P('tensor', 'replica')
- new_weight: bfloat16 [32, 8192, 512], P('replica', 'tensor')
- keys: bfloat16 [32768, 512], P(('replica', 'tensor'))
- grad_tokens: bfloat16 [32768, 8192], P('replica', 'tensor')
- grad_weight: bfloat16 [32, 8192, 512], P('replica', 'tensor')
All inputs are finite; a program needn't handle non-finite values. Where the computation divides by a largest or mean magnitude, that divisor is 1e-20 or more.
Results may differ from a plain program's by a relative error of at most 0.0018.
Values may be sent and summed in bfloat16 or wider, within the bound.
No kernel may reach another device: no remote copies, remote signals or barrier semaphores. Data moves between devices by JAX's collectives and lax.ppermute only.
A program may use at most 64 MiB of HBM per device.

v0:
```python
import jax
import jax.numpy as jnp
from jax import lax
from jax.sharding import PartitionSpec as P

BLOCK = 128


OUTER_RATE = 0.7
MOMENTUM_COEF = 0.9
EPSILON = 1e-06


def body(pseudo_grad, stale_avg, momentum, weight, tokens, cotangent):
    replicas = lax.axis_size("replica")
    replica_index = lax.axis_index("replica")
    owned = momentum.shape[2]
    width = weight.shape[1]
    nblocks = width // BLOCK
    local_rows = pseudo_grad[0]
    local_delta = local_rows.astype(jnp.float32)
    stale_full = stale_avg.astype(jnp.float32)
    stale_owned = lax.dynamic_slice_in_dim(stale_full, replica_index * owned, owned, 0)
    summed_rows = lax.psum_scatter(local_delta, "replica", scatter_dimension=0, tiled=True)
    average_rows = summed_rows / replicas
    moment_next = MOMENTUM_COEF * momentum[0, 0] + stale_owned
    step_owned = (stale_owned + MOMENTUM_COEF * moment_next).astype(jnp.bfloat16)
    step_all = lax.all_gather(step_owned, "replica", axis=0, tiled=True)
    blocks = average_rows.reshape(owned, nblocks, BLOCK)
    scales = jnp.max(jnp.abs(blocks), axis=-1) + EPSILON
    normalized = (blocks / scales[:, :, None]).reshape(owned, width)
    change = step_all.astype(jnp.float32) + (local_delta - stale_full) / replicas
    new_weight = (weight.astype(jnp.float32) - OUTER_RATE * change).astype(jnp.bfloat16)
    rows = tokens
    keys = lax.psum_scatter(
        jnp.dot(rows, weight, preferred_element_type=jnp.float32),
        "tensor",
        scatter_dimension=0,
        tiled=True,
    ).astype(jnp.bfloat16)
    piece = lax.all_gather(cotangent, "tensor", axis=0, tiled=True)
    rows = tokens
    grad_acc = lax.dot_general(
        rows, piece, (((0,), (0,)), ((), ())), preferred_element_type=jnp.float32
    )
    incoming = lax.dot_general(
        piece, weight, (((1,), (1,)), ((), ())), preferred_element_type=jnp.float32
    )
    grad_rows = incoming
    grad_acc, grad_rows = (grad_acc, grad_rows)
    return (
        normalized[None, None],
        scales[None, None],
        moment_next[None, None],
        new_weight[None],
        keys,
        grad_rows.astype(jnp.bfloat16),
        grad_acc.astype(jnp.bfloat16)[None],
    )


def solution(mesh):
    placed = (
        P("replica", "tensor", None),
        P("tensor", None),
        P("tensor", "replica", None, None),
        P("tensor", None),
        P("replica", "tensor"),
        P(("replica", "tensor"), None),
    )
    return jax.shard_map(
        body,
        mesh=mesh,
        in_specs=placed,
        out_specs=(
            P("tensor", "replica", None, None),
            P("tensor", "replica", None, None),
            P("tensor", "replica", None, None),
            P("replica", "tensor", None),
            P(("replica", "tensor"), None),
            P("replica", "tensor"),
            P("replica", "tensor", None),
        ),
        check_vma=False,
    )
```

profile of v0, /device:TPU:16, one launch (start us, length us, event | category | flops | bytes accessed | tf_op | source)
XLA Modules:
  0.0 320.2 jit_solution(3220038647272594315)
XLA Ops:
  8.0 0.0 copy-start
  8.0 0.0 all-gather.2.cloned.1.call-start
  8.1 0.7 all-gather.2.cloned.1.call-update
  8.8 0.0 reduce-scatter.3.cloned.1.call-start
  8.8 2.2 bitcast_convert_fusion
  11.0 0.0 reduce-scatter.3.cloned.1.call-update
  11.0 0.0 copy-start.2
  11.0 0.0 reduce-scatter.5.cloned.1.call-start
  11.1 2.1 fusion.4
  13.1 0.0 reduce-scatter.5.cloned.1.call-update
  13.2 1.1 convert_element_type.32
  14.3 1.4 add_convert_fusion
  15.7 87.6 %all_gather.6 = bf16[512,512]{1,0:T(8,128)(2,1)S(1)} all-gather(bf16[16,512]{1,0:T(8,128)(2,1)S(1)} %get-tuple-element.7), channel_id=1, replica_groups=mesh['replica'=32,'tensor'=16] {'replica'}, dimensions={0}, use_global_device_ids=true | all-gather | bytes 540672 | tf_op jit(solution)/shard_map/all_gather | solution.py:28
  103.2 1.1 fusion.1
  104.4 2.8 fusion
  107.2 1.7 convolution_convert_fusion
  108.9 134.5 %reduce-scatter.3.cloned.1.call-done = f32[16,512]{1,0:T(8,128)} async-done(((f32[512,512]{1,0:T(8,128)}), f32[16,512]{1,0:T(8,128)}) %reduce-scatter.3.cloned.1.call-update) | async-done | bytes 32784 | tf_op jit(solution)/shard_map/reduce_scatter | solution.py:24
  243.4 0.8 multiply_abs_fusion
  244.2 0.1 reduce_max.9
  244.3 0.7 copy.14
  245.0 0.1 div.28
  245.1 1.4 fusion.2
  246.4 64.7 %reduce-scatter.5.cloned.1.call-done = f32[64,512]{1,0:T(8,128)} async-done(((f32[1024,512]{1,0:T(8,128)}), f32[64,512]{1,0:T(8,128)}) %reduce-scatter.5.cloned.1.call-update) | async-done | bytes 131088 | tf_op jit(solution)/shard_map/reduce_scatter | solution.py:35
  311.2 1.5 convert_element_type.37
  (13 shorter events, 0.0 us)
Async XLA Ops:
  8.0 3.1 copy-start
  8.0 3.1 copy-start.3
  8.0 96.3 %all-gather.2.cloned.1.call-start = ((), (), s32[]{:S(2)}) async-start(), calls=%async_computation.4 | async-start | bytes 1114112 | tf_op jit(solution)/shard_map/all_gather | solution.py:41
  8.8 234.7 %reduce-scatter.3.cloned.1.call-start = ((), (), s32[]{:S(2)}) async-start(), calls=%async_computation.2 | async-start | bytes 1081344 | tf_op jit(solution)/shard_map/reduce_scatter | solution.py:24
  11.0 2.2 copy-start.2
  11.0 300.2 %reduce-scatter.5.cloned.1.call-start = ((), (), s32[]{:S(2)}) async-start(), calls=%async_computation.3 | async-start | bytes 2228224 | tf_op jit(solution)/shard_map/reduce_scatter | solution.py:35
  13.1 1.1 copy-start.4
  13.1 90.1 %copy-start.1 = (bf16[1,512,512]{2,1,0:T(8,128)(2,1)S(1)}, bf16[1,512,512]{2,1,0:T(8,128)(2,1)}, u32[]{:S(2)}) copy-start(bf16[1,512,512]{2,1,0:T(8,128)(2,1)} %param.6) | copy-start | bytes 1572868
  104.4 2.8 copy-start.5
Sparse Core Ops, SparseCore 0:
  11.0 42.4 all-gather.1
Sparse Core Ops, SparseCore 1:
  13.6 229.8 reduce-scatter.2
  246.1 65.0 reduce-scatter.4
where the time goes:
time: 321 us; the launch traced here: 320 us
  waiting for transfers between devices  200 us (62%)
  blocking collectives  87.6 us (27%)
  between operations  15.6 us (5%)
  other arithmetic  9.55 us (3%)
  matrix products  6.61 us (2%)
    reduce_scatter x1, waiting for transfers between devices, body(): lax.psum_scatter(local_delta, 'replica', scatter_dimension=0, tiled=True)  135 us
    all_gather x1, blocking collectives, body(): step_all = lax.all_gather(step_owned, 'replica', axis=0, tiled=True)  87.6 us
    reduce_scatter x1, waiting for transfers between devices, body(): lax.psum_scatter(jnp.dot(rows, weight, preferred_element_type=jnp.float32...  64.7 us
  transfers between devices with their start and end apart: 3, of which 2 were waited for; matrix products, arithmetic and copies ran while one was open for 5% of the time, Pallas kernels for 0%

commit v1 on v0

v1 whole, which is shorter than its diff:
```python
import functools

import jax
import jax.numpy as jnp
from jax import lax
from jax.experimental import pallas as pl
from jax.experimental.pallas import tpu as pltpu
from jax.sharding import Mesh, PartitionSpec as P

BLOCK = 128
OUTER_RATE = 0.7
MOMENTUM_COEF = 0.9
EPSILON = 1e-06

REPLICA = ("z", "yh")
TENSOR = ("yl", "x", "core")
CHIPS = ("yl", "x")
SIZES = (8, 4, 2, 4, 2)

EST_PREPARE = 1.0
EST_OWN = 1.0
EST_TAIL = 5.0
EST_GRADS = 1.0

VMEM = pl.BlockSpec(memory_space=pltpu.VMEM)
SMEM = pl.BlockSpec(memory_space=pltpu.SMEM)


def call(kernel, out_shape, ins, us, scratch=()):
    return pl.pallas_call(
        kernel,
        out_shape=out_shape,
        in_specs=ins,
        out_specs=jax.tree.map(lambda _: VMEM, out_shape),
        scratch_shapes=list(scratch),
        compiler_params=pltpu.CompilerParams(vmem_limit_bytes=24 * 1024 * 1024),
        cost_estimate=pl.CostEstimate(
            flops=0, bytes_accessed=int(us * 3.69e6), transcendentals=0
        ),
    )


def prepare_kernel(at, grads, stale, momentum, sent, moment_next):
    owned = momentum.shape[0]
    rows = stale[pl.ds(pl.multiple_of(at[0] * owned, owned), owned), :].astype(jnp.float32)
    moment = MOMENTUM_COEF * momentum[...] + rows
    moment_next[...] = moment
    step = (rows + MOMENTUM_COEF * moment).astype(jnp.bfloat16)
    sent[:, :owned, :] = grads[...]
    sent[:, owned:, :] = jnp.broadcast_to(step[None], grads.shape)


def own_kernel(at, tokens, weight, arrived, kept, *rest):
    outs, held = rest[:-1], rest[-1]
    chips, _, mine, width = tokens.shape
    rows = tokens[:, at[1]].reshape(chips * mine, width)
    part = jnp.dot(rows, weight[...], preferred_element_type=jnp.float32) + arrived[...]
    held[...] = part.reshape(held.shape)
    line = held.shape[1]
    kept[...] = held[:, at[2]]
    for k, out in enumerate(outs):
        out[...] = held[:, lax.rem(at[2] + k + 1, line)]


def grads_kernel(at, tokens, weight, cot_mine, cot_theirs, grad_tokens, grad_weight, held):
    chips, cores, mine, width = held.shape
    held[:, at[1]] = cot_mine[...]
    held[:, 1 - at[1]] = cot_theirs[...]
    cot = held[...].reshape(chips * cores * mine, width)
    grad_tokens[...] = lax.dot_general(
        cot, weight[...], (((1,), (1,)), ((), ())), preferred_element_type=jnp.float32
    ).astype(jnp.bfloat16)
    grad_weight[...] = lax.dot_general(
        tokens[...], cot, (((0,), (0,)), ((), ())), preferred_element_type=jnp.float32
    ).astype(jnp.bfloat16)


def tail_kernel(got, grads, stale, weight, codes, scales, new_weight):
    replicas, twice, width = got.shape
    owned = twice // 2
    total = jnp.sum(got[:, :owned, :].astype(jnp.float32), axis=0)
    average = total / replicas
    parts, largest = [], []
    for b in range(width // BLOCK):
        block = average[:, b * BLOCK:(b + 1) * BLOCK]
        scale = jnp.max(jnp.abs(block), axis=-1, keepdims=True) + EPSILON
        parts.append(block / scale)
        largest.append(scale)
    codes[...] = jnp.concatenate(parts, axis=1)
    scales[...] = jnp.concatenate(largest, axis=1)
    change = got[:, owned:, :].astype(jnp.float32) + (
        grads[...].astype(jnp.float32) - stale[...].astype(jnp.float32)
    ) / replicas
    new_weight[...] = (weight[...].astype(jnp.float32) - OUTER_RATE * change).astype(jnp.bfloat16)


def shift(value, axis, k):
    n = lax.axis_size(axis)
    return lax.ppermute(value, axis, [(i, (i + k) % n) for i in range(n)])


def pick(value, index, axis):
    return lax.dynamic_index_in_dim(value, index, axis, False)


def body(pseudo_grad, stale_avg, momentum, weight, tokens, cotangent):
    replicas = lax.axis_size("z") * lax.axis_size("yh")
    runs, line = lax.axis_size("yl"), lax.axis_size("x")
    chips = runs * line
    core, x_at, yl_at = lax.axis_index("core"), lax.axis_index("x"), lax.axis_index("yl")
    at = jnp.stack([lax.axis_index(REPLICA), core, x_at, yl_at]).astype(jnp.int32)
    owned = momentum.shape[2]
    width = weight.shape[1]
    nblocks = width // BLOCK
    mine = cotangent.shape[0]
    f32, bf16 = jnp.float32, jnp.bfloat16
    struct = jax.ShapeDtypeStruct

    cot_mine = lax.all_to_all(
        jnp.broadcast_to(cotangent[None], (chips, mine, width)), CHIPS, 0, 0
    )

    grouped = tokens.reshape(chips, 2, mine, tokens.shape[1])
    rows_theirs = pick(grouped, 1 - core, 1).reshape(chips * mine, -1)
    arrived = shift(jnp.dot(rows_theirs, weight, preferred_element_type=f32), "core", 1)

    grads = pseudo_grad[0].reshape(replicas, owned, width)
    sent, moment_next = call(
        prepare_kernel,
        [struct((replicas, 2 * owned, width), bf16), struct((owned, width), f32)],
        [SMEM, VMEM, VMEM, VMEM],
        EST_PREPARE,
    )(at, grads, stale_avg, momentum[0, 0])
    got = lax.all_to_all(sent, REPLICA, 0, 0)

    arrived, cot_mine = lax.optimization_barrier((arrived, cot_mine))
    piece = struct((runs, mine, width), f32)
    kept, *pieces = call(
        own_kernel,
        [piece] * line,
        [SMEM, VMEM, VMEM, VMEM],
        EST_OWN,
        [pltpu.VMEM((runs, line, mine, width), f32)],
    )(at, grouped, weight, arrived)
    from_x = [shift(pieces[k - 1], "x", k) for k in (2, 1, 3)]

    cot_theirs = shift(cot_mine, "core", 1)
    grad_tokens, grad_weight = call(
        grads_kernel,
        [struct(tokens.shape, bf16), struct((tokens.shape[1], width), bf16)],
        [SMEM] + [VMEM] * 4,
        EST_GRADS,
        [pltpu.VMEM(grouped.shape, bf16)],
    )(at, tokens, weight, cot_mine, cot_theirs)

    from_x, grad_weight, grad_tokens = lax.optimization_barrier((from_x, grad_weight, grad_tokens))
    acc = kept + from_x[0] + from_x[1] + from_x[2]
    keys = (pick(acc, yl_at, 0) + shift(pick(acc, 1 - yl_at, 0), "yl", 1)).astype(bf16)

    codes, scales, new_weight = call(
        tail_kernel,
        [struct((owned, width), f32), struct((owned, nblocks), f32), struct((replicas, owned, width), bf16)],
        [VMEM] * 4,
        EST_TAIL,
    )(got, grads, stale_avg.reshape(grads.shape), weight.reshape(grads.shape))
    return (
        codes[None, None],
        scales[None, None],
        moment_next[None, None],
        new_weight.reshape(pseudo_grad.shape),
        keys,
        grad_tokens,
        grad_weight[None],
    )


def solution(mesh):
    fine = Mesh(mesh.devices.reshape(SIZES), REPLICA + TENSOR)
    return jax.shard_map(
        body,
        mesh=fine,
        in_specs=(
            P(REPLICA, TENSOR, None),
            P(TENSOR, None),
            P(TENSOR, REPLICA, None, None),
            P(TENSOR, None),
            P(REPLICA, TENSOR),
            P(REPLICA + TENSOR, None),
        ),
        out_specs=(
            P(TENSOR, REPLICA, None, None),
            P(TENSOR, REPLICA, None, None),
            P(TENSOR, REPLICA, None, None),
            P(REPLICA, TENSOR, None),
            P(REPLICA + TENSOR, None),
            P(REPLICA, TENSOR),
            P(REPLICA, TENSOR, None),
        ),
        check_vma=False,
    )
```

time: 321 us -> 68.7 us (0.21)
  the two profiles are of different devices: /device:TPU:16 before, /device:TPU:12 now
where the time goes in v1:
time: 68.7 us; the launch traced here: 68 us
  starting transfers between devices  37.7 us (55%)
  waiting for transfers between devices  11.4 us (17%)
  Pallas kernels  8.47 us (12%)
  local copies, waits for them, and re-layouts  6.32 us (9%)
  other arithmetic  1.92 us (3%)
  matrix products  1.41 us (2%)
  between operations  0.77 us (1%)
    ppermute x6, starting transfers between devices, shift(): return lax.ppermute(value, axis, [(i, (i + k) % n) for i in range(n)])  16.9 us
    all_to_all x1, starting transfers between devices, body(): got = lax.all_to_all(sent, REPLICA, 0, 0)  11.6 us
    all_to_all x1, starting transfers between devices, body(): lax.all_to_all(jnp.broadcast_to(cotangent[None], (chips, mine, width)), C...  9.2 us
    ppermute x6, waiting for transfers between devices, shift(): return lax.ppermute(value, axis, [(i, (i + k) % n) for i in range(n)])  8.33 us
    unnamed x18, local copies, waits for them, and re-layouts  3.85 us
    pallas_call x1, Pallas kernels, body(): call(grads_kernel, [struct(tokens.shape, bf16), struct((tokens.shape[1],...  3.14 us
    all_to_all x1, waiting for transfers between devices, body(): got = lax.all_to_all(sent, REPLICA, 0, 0)  3.04 us
    pallas_call x1, Pallas kernels, body(): call(own_kernel, [piece] * line, [SMEM, VMEM, VMEM, VMEM], EST_OWN, [pltp...  2.62 us
  transfers between devices with their start and end apart: 8, of which 4 were waited for; matrix products, arithmetic and copies ran while one was open for 5% of the time, Pallas kernels for 10%

profile of v1, /device:TPU:12, one launch (start us, length us, event | category | flops | bytes accessed | tf_op | source)
XLA Modules:
  0.0 68.0 jit_solution(9355461106690117500)
XLA Ops:
  0.6 1.8 %broadcast_in_dim.21 = bf16[8,64,512]{2,1,0:T(8,128)(2,1)} broadcast(bf16[64,512]{1,0:T(8,128)(2,1)} %param.11), dimensions={1,2} | broadcast | bytes 589824 | tf_op jit(solution)/shard_map/broadcast_in_dim | solution.py:120
  2.4 9.2 %all-to-all-start.1 = ((bf16[8,64,512]{2,1,0:T(8,128)(2,1)}), bf16[8,64,512]{2,1,0:T(8,128)(2,1)S(1)}, u32[]{:S(2)}, u32[]{:S(2)}) async-start(bf16[8,64,512]{2,1,0:T(8,128)(2,1)} %broadcast_in_dim.21), calls=%async_computation.1 | async-start | bytes 1048576 | tf_op jit(solution)/shard_map/all_to_all | solution.py:119
  11.7 1.0 %copy-done = bf16[512,512]{1,0:T(8,128)(2,1)S(1)} copy-done((bf16[512,512]{1,0:T(8,128)(2,1)S(1)}, bf16[512,512]{1,0:T(8,128)(2,1)}, u32[]{:S(2)}) %copy-start) | copy-done | bytes 524312
  12.7 1.4 %fusion.1 = f32[512,512]{1,0:T(8,128)} fusion(bf16[512,512]{1,0:T(8,128)(2,1)S(1)} %bitcast.30, bf16[512,512]{1,0:T(8,128)(2,1)S(1)} %copy-done), kind=kOutput, calls=%fused_computation.6 | convolution fusion | flops 268435456 | bytes 2097152 | tf_op jit(solution)/shard_map/dot_general | solution.py:125
  14.1 2.0 %collective-permute-start = (f32[512,512]{1,0:T(8,128)}, f32[512,512]{1,0:T(8,128)}, u32[]{:S(2)}, u32[]{:S(2)}) collective-permute-start(f32[512,512]{1,0:T(8,128)} %fusion.1), channel_id=1, source_target_pairs={{0,1},{1,0},{2,3},{3,2},{4,5},{5,4},{6,7},{7,6},{8,9},{9,8},{10,11... | collective-permute-start | bytes 3145736 | tf_op jit(solution)/shard_map/ppermute | solution.py:99
  16.2 1.3 %shard_map.117 = (bf16[32,32,512]{2,1,0:T(8,128)(2,1)S(1)}, f32[16,512]{1,0:T(8,128)}) custom-call(s32[4]{0:T(128)S(1)} %pad_add_fusion.at, bf16[32,16,512]{2,1,0:T(8,128)(2,1)S(1)} %bitcast.26, bf16[512,512]{1,0:T(8,128)(2,1)S(1)} %copy-done.3, f32[16,512]{1,0:T(8,128)S(1)} %bitcast.29), custom_call_target="tpu_custom_call" | custom-call | bytes 3690000 | tf_op jit(solution)/shard_map/pallas_call | solution.py:128
  17.5 1.0 %copy-done.7 = bf16[32,32,512]{2,1,0:T(8,128)(2,1)} copy-done((bf16[32,32,512]{2,1,0:T(8,128)(2,1)}, bf16[32,32,512]{2,1,0:T(8,128)(2,1)S(1)}, u32[]{:S(2)}) %copy-start.7) | copy-done | bytes 1048600
  18.5 0.8 %copy-done.5 = bf16[8,64,512]{2,1,0:T(8,128)(2,1)} copy-done((bf16[8,64,512]{2,1,0:T(8,128)(2,1)}, bf16[8,64,512]{2,1,0:T(8,128)(2,1)S(1)}, u32[]{:S(2)}) %copy-start.5) | copy-done | bytes 524312
  19.3 11.6 %all-to-all-start = ((bf16[32,32,512]{2,1,0:T(8,128)(2,1)}), bf16[32,32,512]{2,1,0:T(8,128)(2,1)S(1)}, u32[]{:S(2)}, u32[]{:S(2)}) async-start(bf16[32,32,512]{2,1,0:T(8,128)(2,1)} %copy-done.7), calls=%async_computation | async-start | bytes 2097152 | tf_op jit(solution)/shard_map/all_to_all | solution.py:134
  30.9 2.1 %collective-permute-start.4 = (bf16[8,64,512]{2,1,0:T(8,128)(2,1)}, bf16[8,64,512]{2,1,0:T(8,128)(2,1)}, u32[]{:S(2)}, u32[]{:S(2)}) collective-permute-start(bf16[8,64,512]{2,1,0:T(8,128)(2,1)} %copy-done.5), channel_id=1, source_target_pairs={{0,1},{1,0},{2,3},{3,2},{4,5},{5,4},{6,7},{7,6},{8,9},{9,8},{10,11... | collective-permute-start | bytes 1572872 | tf_op jit(solution)/shard_map/ppermute | solution.py:99
  33.0 2.6 %shard_map.119 = (f32[2,64,512]{2,1,0:T(8,128)S(1)}, f32[2,64,512]{2,1,0:T(8,128)}, f32[2,64,512]{2,1,0:T(8,128)}, f32[2,64,512]{2,1,0:T(8,128)}) custom-call(s32[4]{0:T(128)S(1)} %pad_add_fusion.at, bf16[8,2,64,512]{3,2,1,0:T(8,128)(2,1)S(1)} %bitcast.25, bf16[512,512]{1,0:T(8,128)(2,1)S(1)} %copy-done, f32[512,512]{1,0:T(8,128)} %collective-permute-done.arrived), custom_call_target="tpu_custom_call" | custom-call | bytes 3690000 | tf_op jit(solution)/shard_map/pallas_call | solution.py:138
  35.6 4.0 %collective-permute-start.1 = (f32[2,64,512]{2,1,0:T(8,128)}, f32[2,64,512]{2,1,0:T(8,128)}, u32[]{:S(2)}, u32[]{:S(2)}) collective-permute-start(f32[2,64,512]{2,1,0:T(8,128)} %get-tuple-element.32), channel_id=1, source_target_pairs={{0,4},{2,6},{4,0},{6,2},{1,5},{3,7},{5,1},{7,3},{8,12},{10,14},{12... | collective-permute-start | bytes 786440 | tf_op jit(solution)/shard_map/ppermute | solution.py:99
  39.6 3.4 %collective-permute-start.2 = (f32[2,64,512]{2,1,0:T(8,128)}, f32[2,64,512]{2,1,0:T(8,128)}, u32[]{:S(2)}, u32[]{:S(2)}) collective-permute-start(f32[2,64,512]{2,1,0:T(8,128)} %get-tuple-element.33), channel_id=1, source_target_pairs={{0,2},{2,4},{4,6},{6,0},{1,3},{3,5},{5,7},{7,1},{8,10},{10,12},{12... | collective-permute-start | bytes 786440 | tf_op jit(solution)/shard_map/ppermute | solution.py:99
  43.0 2.5 %collective-permute-start.3 = (f32[2,64,512]{2,1,0:T(8,128)}, f32[2,64,512]{2,1,0:T(8,128)}, u32[]{:S(2)}, u32[]{:S(2)}) collective-permute-start(f32[2,64,512]{2,1,0:T(8,128)} %get-tuple-element.34), channel_id=1, source_target_pairs={{0,6},{2,0},{4,2},{6,4},{1,7},{3,1},{5,3},{7,5},{8,14},{10,8},{12,... | collective-permute-start | bytes 786440 | tf_op jit(solution)/shard_map/ppermute | solution.py:99
  45.5 1.0 %copy-done.6 = bf16[8,64,512]{2,1,0:T(8,128)(2,1)S(1)} copy-done((bf16[8,64,512]{2,1,0:T(8,128)(2,1)S(1)}, bf16[8,64,512]{2,1,0:T(8,128)(2,1)}, u32[]{:S(2)}) %copy-start.6) | copy-done | bytes 524312
  46.6 3.1 %shard_map.120 = (bf16[1024,512]{1,0:T(8,128)(2,1)}, bf16[512,512]{1,0:T(8,128)(2,1)}) custom-call(s32[4]{0:T(128)S(1)} %pad_add_fusion.at, bf16[1024,512]{1,0:T(8,128)(2,1)S(1)} %copy-done.1, bf16[512,512]{1,0:T(8,128)(2,1)S(1)} %copy-done, bf16[8,64,512]{2,1,0:T(8,128)(2,1)S(1)} %copy-done.6, bf16[8,64,512]{2,1,0:T(8,128)(2,1)} %collective-permute-done.4.cot_theirs), custom_call_target="tpu_custom_call" | custom-call | bytes 3690000 | tf_op jit(solution)/shard_map/pallas_call | solution.py:148
  49.7 3.8 %collective-permute-done.2 = f32[2,64,512]{2,1,0:T(8,128)} collective-permute-done((f32[2,64,512]{2,1,0:T(8,128)}, f32[2,64,512]{2,1,0:T(8,128)}, u32[]{:S(2)}, u32[]{:S(2)}) %collective-permute-start.2) | collective-permute-done | bytes 262176 | tf_op jit(solution)/shard_map/ppermute | solution.py:99
  53.7 1.2 %add_add_fusion = f32[2,64,512]{2,1,0:T(8,128)S(1)} fusion(f32[2,64,512]{2,1,0:T(8,128)} %collective-permute-done.3, f32[2,64,512]{2,1,0:T(8,128)} %collective-permute-done.2, f32[2,64,512]{2,1,0:T(8,128)S(1)} %get-tuple-element.31, f32[2,64,512]{2,1,0:T(8,128)} %collective-permute-done.1), kind=kLoop, calls=%fused_computation | loop fusion | flops 196608 | bytes 1310720 | tf_op jit(solution)/shard_map/add | solution.py:157
  54.9 2.9 %collective-permute-start.5 = (f32[64,512]{1,0:T(8,128)S(1)}, f32[64,512]{1,0:T(8,128)S(1)}, u32[]{:S(2)}, u32[]{:S(2)}) collective-permute-start(f32[64,512]{1,0:T(8,128)S(1)} %dynamic-slice_bitcast_fusion), channel_id=1, source_target_pairs={{0,8},{8,0},{1,9},{9,1},{2,10},{10,2},{3,11},{11,3},{4,12},{12,4},... | collective-permute-start | bytes 393224 | tf_op jit(solution)/shard_map/ppermute | solution.py:99
  57.8 4.3 %collective-permute-done.5 = f32[64,512]{1,0:T(8,128)S(1)} collective-permute-done((f32[64,512]{1,0:T(8,128)S(1)}, f32[64,512]{1,0:T(8,128)S(1)}, u32[]{:S(2)}, u32[]{:S(2)}) %collective-permute-start.5) | collective-permute-done | bytes 131104 | tf_op jit(solution)/shard_map/ppermute | solution.py:99
  62.2 0.6 fusion
  62.8 3.0 %all-to-all-done.got = bf16[32,32,512]{2,1,0:T(8,128)(2,1)S(1)} async-done(((bf16[32,32,512]{2,1,0:T(8,128)(2,1)}), bf16[32,32,512]{2,1,0:T(8,128)(2,1)S(1)}, u32[]{:S(2)}, u32[]{:S(2)}) %all-to-all-start) | async-done | bytes 1048608 | tf_op jit(solution)/shard_map/all_to_all | solution.py:134
  65.9 1.4 %shard_map.118 = (f32[16,512]{1,0:T(8,128)}, f32[16,4]{1,0:T(8,128)S(1)}, bf16[32,16,512]{2,1,0:T(8,128)(2,1)}) custom-call(bf16[32,32,512]{2,1,0:T(8,128)(2,1)S(1)} %all-to-all-done.got, bf16[32,16,512]{2,1,0:T(8,128)(2,1)S(1)} %bitcast.27, bf16[32,16,512]{2,1,0:T(8,128)(2,1)S(1)} %bitcast.28, bf16[32,16,512]{2,1,0:T(8,128)(2,1)S(1)} %bitcast.23), custom_call_target="tpu_custom_call" | custom-call | bytes 18450000 | tf_op jit(solution)/shard_map/pallas_call | solution.py:160
  67.3 0.7 copy.13
  (22 shorter events, 0.4 us)
Async XLA Ops:
  0.6 11.0 %copy-start.1 = (bf16[1024,512]{1,0:T(8,128)(2,1)S(1)}, bf16[1024,512]{1,0:T(8,128)(2,1)}, u32[]{:S(2)}) copy-start(bf16[1024,512]{1,0:T(8,128)(2,1)} %tokens.1) | copy-start | bytes 3145732
  2.4 16.1 %all-to-all-start.1 = ((bf16[8,64,512]{2,1,0:T(8,128)(2,1)}), bf16[8,64,512]{2,1,0:T(8,128)(2,1)S(1)}, u32[]{:S(2)}, u32[]{:S(2)}) async-start(bf16[8,64,512]{2,1,0:T(8,128)(2,1)} %broadcast_in_dim.21), calls=%async_computation.1 | async-start | bytes 1048576 | tf_op jit(solution)/shard_map/all_to_all | solution.py:119
  11.6 1.0 %copy-start = (bf16[512,512]{1,0:T(8,128)(2,1)S(1)}, bf16[512,512]{1,0:T(8,128)(2,1)}, u32[]{:S(2)}) copy-start(bf16[512,512]{1,0:T(8,128)(2,1)} %weight.3) | copy-start | bytes 1572868
  12.6 3.6 %copy-start.2 = (bf16[1,512,512]{2,1,0:T(8,128)(2,1)S(1)}, bf16[1,512,512]{2,1,0:T(8,128)(2,1)}, u32[]{:S(2)}) copy-start(bf16[1,512,512]{2,1,0:T(8,128)(2,1)} %param.6) | copy-start | bytes 1572868
  12.6 3.6 %copy-start.3 = (bf16[512,512]{1,0:T(8,128)(2,1)S(1)}, bf16[512,512]{1,0:T(8,128)(2,1)}, u32[]{:S(2)}) copy-start(bf16[512,512]{1,0:T(8,128)(2,1)} %stale.1) | copy-start | bytes 1572868
  14.1 2.1 %copy-start.8 = (f32[1,1,16,512]{3,2,1,0:T(8,128)S(1)}, f32[1,1,16,512]{3,2,1,0:T(8,128)}, u32[]{:S(2)}) copy-start(f32[1,1,16,512]{3,2,1,0:T(8,128)} %param.8) | copy-start | bytes 98308
  14.1 16.8 %collective-permute-start = (f32[512,512]{1,0:T(8,128)}, f32[512,512]{1,0:T(8,128)}, u32[]{:S(2)}, u32[]{:S(2)}) collective-permute-start(f32[512,512]{1,0:T(8,128)} %fusion.1), channel_id=1, source_target_pairs={{0,1},{1,0},{2,3},{3,2},{4,5},{5,4},{6,7},{7,6},{8,9},{9,8},{10,11... | collective-permute-start | bytes 3145736 | tf_op jit(solution)/shard_map/ppermute | solution.py:99
  17.5 1.0 %copy-start.7 = (bf16[32,32,512]{2,1,0:T(8,128)(2,1)}, bf16[32,32,512]{2,1,0:T(8,128)(2,1)S(1)}, u32[]{:S(2)}) copy-start(bf16[32,32,512]{2,1,0:T(8,128)(2,1)S(1)} %get-tuple-element.25) | copy-start | bytes 3145732
  18.5 0.8 %copy-start.5 = (bf16[8,64,512]{2,1,0:T(8,128)(2,1)}, bf16[8,64,512]{2,1,0:T(8,128)(2,1)S(1)}, u32[]{:S(2)}) copy-start(bf16[8,64,512]{2,1,0:T(8,128)(2,1)S(1)} %all-to-all-done.1.cot_mine) | copy-start | bytes 1572868
  19.3 46.6 %all-to-all-start = ((bf16[32,32,512]{2,1,0:T(8,128)(2,1)}), bf16[32,32,512]{2,1,0:T(8,128)(2,1)S(1)}, u32[]{:S(2)}, u32[]{:S(2)}) async-start(bf16[32,32,512]{2,1,0:T(8,128)(2,1)} %copy-done.7), calls=%async_computation | async-start | bytes 2097152 | tf_op jit(solution)/shard_map/all_to_all | solution.py:134
  30.9 14.6 %collective-permute-start.4 = (bf16[8,64,512]{2,1,0:T(8,128)(2,1)}, bf16[8,64,512]{2,1,0:T(8,128)(2,1)}, u32[]{:S(2)}, u32[]{:S(2)}) collective-permute-start(bf16[8,64,512]{2,1,0:T(8,128)(2,1)} %copy-done.5), channel_id=1, source_target_pairs={{0,1},{1,0},{2,3},{3,2},{4,5},{5,4},{6,7},{7,6},{8,9},{9,8},{10,11... | collective-permute-start | bytes 1572872 | tf_op jit(solution)/shard_map/ppermute | solution.py:99
  35.6 14.1 %collective-permute-start.1 = (f32[2,64,512]{2,1,0:T(8,128)}, f32[2,64,512]{2,1,0:T(8,128)}, u32[]{:S(2)}, u32[]{:S(2)}) collective-permute-start(f32[2,64,512]{2,1,0:T(8,128)} %get-tuple-element.32), channel_id=1, source_target_pairs={{0,4},{2,6},{4,0},{6,2},{1,5},{3,7},{5,1},{7,3},{8,12},{10,14},{12... | collective-permute-start | bytes 786440 | tf_op jit(solution)/shard_map/ppermute | solution.py:99
  39.6 13.8 %collective-permute-start.2 = (f32[2,64,512]{2,1,0:T(8,128)}, f32[2,64,512]{2,1,0:T(8,128)}, u32[]{:S(2)}, u32[]{:S(2)}) collective-permute-start(f32[2,64,512]{2,1,0:T(8,128)} %get-tuple-element.33), channel_id=1, source_target_pairs={{0,2},{2,4},{4,6},{6,0},{1,3},{3,5},{5,7},{7,1},{8,10},{10,12},{12... | collective-permute-start | bytes 786440 | tf_op jit(solution)/shard_map/ppermute | solution.py:99
  43.0 10.7 %collective-permute-start.3 = (f32[2,64,512]{2,1,0:T(8,128)}, f32[2,64,512]{2,1,0:T(8,128)}, u32[]{:S(2)}, u32[]{:S(2)}) collective-permute-start(f32[2,64,512]{2,1,0:T(8,128)} %get-tuple-element.34), channel_id=1, source_target_pairs={{0,6},{2,0},{4,2},{6,4},{1,7},{3,1},{5,3},{7,5},{8,14},{10,8},{12,... | collective-permute-start | bytes 786440 | tf_op jit(solution)/shard_map/ppermute | solution.py:99
  45.5 1.0 %copy-start.6 = (bf16[8,64,512]{2,1,0:T(8,128)(2,1)S(1)}, bf16[8,64,512]{2,1,0:T(8,128)(2,1)}, u32[]{:S(2)}) copy-start(bf16[8,64,512]{2,1,0:T(8,128)(2,1)} %copy-done.5) | copy-start | bytes 1572868
  54.9 11.0 %copy-start.4 = (bf16[512,512]{1,0:T(8,128)(2,1)S(1)}, bf16[512,512]{1,0:T(8,128)(2,1)}, u32[]{:S(2)}) copy-start(bf16[512,512]{1,0:T(8,128)(2,1)} %stale.1) | copy-start | bytes 1572868
  54.9 7.2 %collective-permute-start.5 = (f32[64,512]{1,0:T(8,128)S(1)}, f32[64,512]{1,0:T(8,128)S(1)}, u32[]{:S(2)}, u32[]{:S(2)}) collective-permute-start(f32[64,512]{1,0:T(8,128)S(1)} %dynamic-slice_bitcast_fusion), channel_id=1, source_target_pairs={{0,8},{8,0},{1,9},{9,1},{2,10},{10,2},{3,11},{11,3},{4,12},{12,4},... | collective-permute-start | bytes 393224 | tf_op jit(solution)/shard_map/ppermute | solution.py:99

commit v2 on v1

v2 whole, which is shorter than its diff:
```python
import jax
import jax.numpy as jnp
from jax import lax
from jax.experimental import pallas as pl
from jax.experimental.pallas import tpu as pltpu
from jax.sharding import Mesh, PartitionSpec as P

BLOCK = 128
OUTER_RATE = 0.7
MOMENTUM_COEF = 0.9
EPSILON = 1e-06

REPLICA = ("z", "yh")
TENSOR = ("yl", "x", "core")
CHIPS = ("yl", "x")
SIZES = (8, 4, 2, 4, 2)

MIB = 1024 * 1024
VMEM = pl.BlockSpec(memory_space=pltpu.VMEM)
SMEM = pl.BlockSpec(memory_space=pltpu.SMEM)
HBM = pl.BlockSpec(memory_space=pltpu.HBM)
F32, BF16 = jnp.float32, jnp.bfloat16
struct = jax.ShapeDtypeStruct


def call(kernel, ins, outs, moved, flops, scratch=(), limit=8 * MIB):
    return pl.pallas_call(
        kernel,
        out_shape=[struct(shape, dtype) for shape, dtype, _ in outs],
        in_specs=ins,
        out_specs=[spec for _, _, spec in outs],
        scratch_shapes=list(scratch),
        compiler_params=pltpu.CompilerParams(vmem_limit_bytes=limit),
        cost_estimate=pl.CostEstimate(flops=flops, bytes_accessed=moved, transcendentals=0),
    )


def spread_kernel(rows, out, sems):
    copies = [pltpu.make_async_copy(rows, out.at[i], sems.at[i]) for i in range(out.shape[0])]
    for copy in copies:
        copy.start()
    for copy in copies:
        copy.wait()


def front_kernel(at, grads, stale, momentum, tokens, weight, sent, moment_next, theirs, rows, step, other, sems):
    owned = momentum.shape[0]
    chips, mine, width = other.shape
    copy_rows = pltpu.make_async_copy(
        stale.at[pl.ds(pl.multiple_of(at[0] * owned, owned), owned), :], rows, sems.at[0]
    )
    copy_tokens = pltpu.make_async_copy(tokens.at[:, 1 - at[1]], other, sems.at[1])
    copy_grads = pltpu.make_async_copy(grads, sent.at[:, :owned, :], sems.at[2])
    copy_step = pltpu.make_async_copy(step, sent.at[:, owned:, :], sems.at[3])
    copy_rows.start()
    copy_tokens.start()
    copy_grads.start()
    copy_rows.wait()
    old = rows[...].astype(F32)
    moment = MOMENTUM_COEF * momentum[...] + old
    moment_next[...] = moment
    step[...] = jnp.broadcast_to((old + MOMENTUM_COEF * moment).astype(BF16)[None], step.shape)
    copy_step.start()
    copy_tokens.wait()
    theirs[...] = jnp.dot(
        other[...].reshape(chips * mine, width), weight[...], preferred_element_type=F32
    )
    copy_grads.wait()
    copy_step.wait()


def own_kernel(at, tokens, weight, arrived, *outs):
    runs, mine, width = outs[0].shape
    line = len(outs)
    for k, out in enumerate(outs):
        x = lax.rem(at[2] + k, line)
        rows = jnp.concatenate([tokens[y * line + x, at[1]] for y in range(runs)], axis=0)
        part = jnp.dot(rows, weight[...], preferred_element_type=F32)
        for y in range(runs):
            out[y] = part[y * mine:(y + 1) * mine] + arrived[y * line + x]


def grads_kernel(at, tokens, weight, cot_mine, cot_theirs, grad_tokens, grad_weight, held, sems):
    chips, cores, mine, width = held.shape
    copies = [
        pltpu.make_async_copy(cot_mine, held.at[:, at[1]], sems.at[0]),
        pltpu.make_async_copy(cot_theirs, held.at[:, 1 - at[1]], sems.at[1]),
    ]
    for copy in copies:
        copy.start()
    for copy in copies:
        copy.wait()
    cot = held[...].reshape(chips * cores * mine, width)
    grad_tokens[...] = lax.dot_general(
        cot, weight[...], (((1,), (1,)), ((), ())), preferred_element_type=F32
    ).astype(BF16)
    grad_weight[...] = lax.dot_general(
        tokens[...], cot, (((0,), (0,)), ((), ())), preferred_element_type=F32
    ).astype(BF16)


def tail_kernel(got, grads, stale, weight, here, there, codes, scales, new_weight, keys):
    replicas, twice, width = got.shape
    owned = twice // 2
    total = jnp.sum(got[:, :owned, :].astype(F32), axis=0)
    average = total / replicas
    diagonal = lax.broadcasted_iota(jnp.int32, (owned, owned), 0) == lax.broadcasted_iota(
        jnp.int32, (owned, owned), 1
    )
    for b in range(width // BLOCK):
        columns = slice(b * BLOCK, (b + 1) * BLOCK)
        block = average[:, columns]
        scale = jnp.max(jnp.abs(block), axis=-1, keepdims=True) + EPSILON
        codes[:, columns] = block / scale
        scales[b:b + 1, :] = jnp.sum(jnp.where(diagonal, scale, 0.0), axis=0, keepdims=True)
    change = got[:, owned:, :].astype(F32) + (grads[...].astype(F32) - stale[...].astype(F32)) / replicas
    new_weight[...] = (weight[...].astype(F32) - OUTER_RATE * change).astype(BF16)
    keys[...] = (here[...] + there[...]).astype(BF16)


def shift(value, axis, k):
    n = lax.axis_size(axis)
    return lax.ppermute(value, axis, [(i, (i + k) % n) for i in range(n)])


def pick(value, index, axis):
    return lax.dynamic_index_in_dim(value, index, axis, False)


def body(pseudo_grad, stale_avg, momentum, weight, tokens, cotangent):
    replicas = lax.axis_size("z") * lax.axis_size("yh")
    runs, line = lax.axis_size("yl"), lax.axis_size("x")
    chips = runs * line
    core, x_at, yl_at = lax.axis_index("core"), lax.axis_index("x"), lax.axis_index("yl")
    at = jnp.stack([lax.axis_index(REPLICA), core, x_at, yl_at]).astype(jnp.int32)
    owned = momentum.shape[2]
    rows, width = weight.shape
    nblocks = width // BLOCK
    mine = cotangent.shape[0]
    dma = pltpu.SemaphoreType.DMA
    block = rows * width

    (copies,) = call(
        spread_kernel,
        [VMEM],
        [((chips, mine, width), BF16, HBM)],
        4 * cotangent.size * chips,
        0,
        [dma((chips,))],
    )(cotangent)
    cot_mine = lax.all_to_all(copies, CHIPS, 0, 0)

    grads = pseudo_grad[0].reshape(replicas, owned, width)
    grouped = tokens.reshape(chips, 2, mine, rows)
    sent, moment_next, theirs = call(
        front_kernel,
        [SMEM, HBM, HBM, VMEM, HBM, VMEM],
        [
            ((replicas, 2 * owned, width), BF16, HBM),
            ((owned, width), F32, VMEM),
            ((chips * mine, width), F32, VMEM),
        ],
        12 * block,
        0,
        [
            pltpu.VMEM((owned, width), BF16),
            pltpu.VMEM((replicas, owned, width), BF16),
            pltpu.VMEM((chips, mine, rows), BF16),
            dma((4,)),
        ],
    )(at, grads, stale_avg, momentum[0, 0], grouped, weight)
    arrived = shift(theirs, "core", 1).reshape(chips, mine, width)
    got = lax.all_to_all(sent, REPLICA, 0, 0)

    arrived, cot_mine = lax.optimization_barrier((arrived, cot_mine))
    kept, *pieces = call(
        own_kernel,
        [SMEM, VMEM, VMEM, VMEM],
        [((runs, mine, width), F32, VMEM)] * line,
        10 * block,
        0,
    )(at, grouped, weight, arrived)
    from_x = [shift(pieces[k - 1], "x", k) for k in (2, 1, 3)]

    cot_theirs = shift(cot_mine, "core", 1)
    grad_tokens, grad_weight = call(
        grads_kernel,
        [SMEM, VMEM, VMEM, HBM, HBM],
        [(tokens.shape, BF16, VMEM), ((rows, width), BF16, VMEM)],
        12 * block,
        0,
        [pltpu.VMEM(grouped.shape, BF16), dma((2,))],
        16 * MIB,
    )(at, tokens, weight, cot_mine, cot_theirs)

    from_x, grad_weight, grad_tokens = lax.optimization_barrier((from_x, grad_weight, grad_tokens))
    acc = kept + from_x[0] + from_x[1] + from_x[2]
    there = shift(pick(acc, 1 - yl_at, 0), "yl", 1)

    codes, scales, new_weight, keys = call(
        tail_kernel,
        [VMEM] * 6,
        [
            ((owned, width), F32, VMEM),
            ((nblocks, owned), F32, VMEM),
            ((replicas, owned, width), BF16, VMEM),
            ((mine, width), BF16, VMEM),
        ],
        12 * block,
        0,
        limit=12 * MIB,
    )(got, grads, stale_avg.reshape(grads.shape), weight.reshape(grads.shape), pick(acc, yl_at, 0), there)
    return (
        codes[None, None],
        scales.T[None, None],
        moment_next[None, None],
        new_weight.reshape(pseudo_grad.shape),
        keys,
        grad_tokens,
        grad_weight[None],
    )


def solution(mesh):
    fine = Mesh(mesh.devices.reshape(SIZES), REPLICA + TENSOR)
    return jax.shard_map(
        body,
        mesh=fine,
        in_specs=(
            P(REPLICA, TENSOR, None),
            P(TENSOR, None),
            P(TENSOR, REPLICA, None, None),
            P(TENSOR, None),
            P(REPLICA, TENSOR),
            P(REPLICA + TENSOR, None),
        ),
        out_specs=(
            P(TENSOR, REPLICA, None, None),
            P(TENSOR, REPLICA, None, None),
            P(TENSOR, REPLICA, None, None),
            P(REPLICA, TENSOR, None),
            P(REPLICA + TENSOR, None),
            P(REPLICA, TENSOR),
            P(REPLICA, TENSOR, None),
        ),
        check_vma=False,
    )
```

time: 68.7 us -> 66.2 us (0.964)
  the two profiles are of different devices: /device:TPU:12 before, /device:TPU:40 now
where the time goes in v2:
time: 66.2 us; the launch traced here: 65.5 us
  starting transfers between devices  39.9 us (60%)
  Pallas kernels  10.7 us (16%)
  waiting for transfers between devices  8.09 us (12%)
  local copies, waits for them, and re-layouts  4.71 us (7%)
  other arithmetic  1.33 us (2%)
  between operations  0.8 us (1%)
    ppermute x6, starting transfers between devices, shift(): return lax.ppermute(value, axis, [(i, (i + k) % n) for i in range(n)])  18.1 us
    all_to_all x1, starting transfers between devices, body(): got = lax.all_to_all(sent, REPLICA, 0, 0)  15.8 us
    ppermute x6, waiting for transfers between devices, shift(): return lax.ppermute(value, axis, [(i, (i + k) % n) for i in range(n)])  7.44 us
    all_to_all x1, starting transfers between devices, body(): cot_mine = lax.all_to_all(copies, CHIPS, 0, 0)  5.9 us
    unnamed x18, local copies, waits for them, and re-layouts  4.69 us
    pallas_call x1, Pallas kernels, body(): call(grads_kernel, [SMEM, VMEM, VMEM, HBM, HBM], [(tokens.shape, BF16, VM...  3.72 us
    pallas_call x1, Pallas kernels, body(): call(own_kernel, [SMEM, VMEM, VMEM, VMEM], [((runs, mine, width), F32, VM...  2.42 us
    pallas_call x1, Pallas kernels, body(): call(front_kernel, [SMEM, HBM, HBM, VMEM, HBM, VMEM], [((replicas, 2 * ow...  2.22 us
  transfers between devices with their start and end apart: 8, of which 3 were waited for; matrix products, arithmetic and copies ran while one was open for 2% of the time, Pallas kernels for 13%

profile of v2, /device:TPU:40, one launch (start us, length us, event | category | flops | bytes accessed | tf_op | source)
XLA Modules:
  0.0 65.5 jit_solution(17911474053195995332)
XLA Ops:
  0.7 0.9 %copy-done.7 = bf16[64,512]{1,0:T(8,128)(2,1)S(1)} copy-done((bf16[64,512]{1,0:T(8,128)(2,1)S(1)}, bf16[64,512]{1,0:T(8,128)(2,1)}, u32[]{:S(2)}) %copy-start.7) | copy-done | bytes 65560
  1.6 0.8 %shard_map.118 = bf16[8,64,512]{2,1,0:T(8,128)(2,1)} custom-call(bf16[64,512]{1,0:T(8,128)(2,1)S(1)} %copy-done.7), custom_call_target="tpu_custom_call" | custom-call | bytes 1048576 | tf_op jit(solution)/shard_map/pallas_call | solution.py:143
  2.4 0.0 copy-start.1
  2.4 5.9 %all-to-all-start.1 = ((bf16[8,64,512]{2,1,0:T(8,128)(2,1)}), bf16[8,64,512]{2,1,0:T(8,128)(2,1)S(1)}, u32[]{:S(2)}, u32[]{:S(2)}) async-start(bf16[8,64,512]{2,1,0:T(8,128)(2,1)} %shard_map.118), calls=%async_computation.1 | async-start | bytes 1048576 | tf_op jit(solution)/shard_map/all_to_all | solution.py:151
  8.3 0.1 pad_add_fusion.at
  8.4 0.7 %copy-done.8 = f32[1,1,16,512]{3,2,1,0:T(8,128)S(1)} copy-done((f32[1,1,16,512]{3,2,1,0:T(8,128)S(1)}, f32[1,1,16,512]{3,2,1,0:T(8,128)}, u32[]{:S(2)}) %copy-start.8) | copy-done | bytes 32792
  9.1 1.0 %copy-done.2 = bf16[1,512,512]{2,1,0:T(8,128)(2,1)S(1)} copy-done((bf16[1,512,512]{2,1,0:T(8,128)(2,1)S(1)}, bf16[1,512,512]{2,1,0:T(8,128)(2,1)}, u32[]{:S(2)}) %copy-start.2) | copy-done | bytes 524312
  10.1 1.0 %copy-done.4 = bf16[512,512]{1,0:T(8,128)(2,1)S(1)} copy-done((bf16[512,512]{1,0:T(8,128)(2,1)S(1)}, bf16[512,512]{1,0:T(8,128)(2,1)}, u32[]{:S(2)}) %copy-start.4) | copy-done | bytes 524312
  11.2 2.2 %shard_map.117 = (bf16[32,32,512]{2,1,0:T(8,128)(2,1)S(1)}, f32[16,512]{1,0:T(8,128)}, f32[512,512]{1,0:T(8,128)}) custom-call(s32[4]{0:T(128)S(1)} %pad_add_fusion.at, bf16[32,16,512]{2,1,0:T(8,128)(2,1)S(1)} %bitcast.24, bf16[512,512]{1,0:T(8,128)(2,1)S(1)} %copy-done.4, f32[16,512]{1,0:T(8,128)S(1)} %bitcast.27, bf16[8,2,64,512]{3,2,1,0:T(8,128)(2,1)S(1)} %bitcast.21, ...), custom_call_target="tpu_custom_call" | custom-call | bytes 3145728 | tf_op jit(solution)/shard_map/pallas_call | solution.py:155
  13.4 1.0 %copy-done.6 = bf16[32,32,512]{2,1,0:T(8,128)(2,1)} copy-done((bf16[32,32,512]{2,1,0:T(8,128)(2,1)}, bf16[32,32,512]{2,1,0:T(8,128)(2,1)S(1)}, u32[]{:S(2)}) %copy-start.6) | copy-done | bytes 1048600
  14.4 1.9 %collective-permute-start = (f32[512,512]{1,0:T(8,128)}, f32[512,512]{1,0:T(8,128)}, u32[]{:S(2)}, u32[]{:S(2)}) collective-permute-start(f32[512,512]{1,0:T(8,128)} %get-tuple-element.28), channel_id=1, source_target_pairs={{0,1},{1,0},{2,3},{3,2},{4,5},{5,4},{6,7},{7,6},{8,9},{9,8},{10,11... | collective-permute-start | bytes 3145736 | tf_op jit(solution)/shard_map/ppermute | solution.py:123
  16.3 0.6 all-to-all-done.1.cot_mine
  17.0 15.8 %all-to-all-start = ((bf16[32,32,512]{2,1,0:T(8,128)(2,1)}), bf16[32,32,512]{2,1,0:T(8,128)(2,1)S(1)}, u32[]{:S(2)}, u32[]{:S(2)}) async-start(bf16[32,32,512]{2,1,0:T(8,128)(2,1)} %copy-done.6), calls=%async_computation | async-start | bytes 2097152 | tf_op jit(solution)/shard_map/all_to_all | solution.py:173
  32.8 1.9 %collective-permute-start.4 = (bf16[8,64,512]{2,1,0:T(8,128)(2,1)S(1)}, bf16[8,64,512]{2,1,0:T(8,128)(2,1)}, u32[]{:S(2)}, u32[]{:S(2)}) collective-permute-start(bf16[8,64,512]{2,1,0:T(8,128)(2,1)S(1)} %all-to-all-done.1.cot_mine), channel_id=1, source_target_pairs={{0,1},{1,0},{2,3},{3,2},{4,5},{5,4},{6,7},{7,6},{8,9},{9,8},{10,11... | collective-permute-start | bytes 1572872 | tf_op jit(solution)/shard_map/ppermute | solution.py:123
  34.8 2.4 %shard_map.119 = (f32[2,64,512]{2,1,0:T(8,128)S(1)}, f32[2,64,512]{2,1,0:T(8,128)}, f32[2,64,512]{2,1,0:T(8,128)}, f32[2,64,512]{2,1,0:T(8,128)}) custom-call(s32[4]{0:T(128)S(1)} %pad_add_fusion.at, bf16[8,2,64,512]{3,2,1,0:T(8,128)(2,1)S(1)} %bitcast.22, bf16[512,512]{1,0:T(8,128)(2,1)S(1)} %copy-done.1, f32[8,64,512]{2,1,0:T(8,128)} %bitcast.9.arrived), custom_call_target="tpu_custom_call" | custom-call | bytes 2621440 | tf_op jit(solution)/shard_map/pallas_call | solution.py:176
  37.2 4.2 %collective-permute-start.1 = (f32[2,64,512]{2,1,0:T(8,128)}, f32[2,64,512]{2,1,0:T(8,128)}, u32[]{:S(2)}, u32[]{:S(2)}) collective-permute-start(f32[2,64,512]{2,1,0:T(8,128)} %get-tuple-element.31), channel_id=1, source_target_pairs={{0,4},{2,6},{4,0},{6,2},{1,5},{3,7},{5,1},{7,3},{8,12},{10,14},{12... | collective-permute-start | bytes 786440 | tf_op jit(solution)/shard_map/ppermute | solution.py:123
  41.4 2.5 %collective-permute-start.2 = (f32[2,64,512]{2,1,0:T(8,128)}, f32[2,64,512]{2,1,0:T(8,128)}, u32[]{:S(2)}, u32[]{:S(2)}) collective-permute-start(f32[2,64,512]{2,1,0:T(8,128)} %get-tuple-element.32), channel_id=1, source_target_pairs={{0,2},{2,4},{4,6},{6,0},{1,3},{3,5},{5,7},{7,1},{8,10},{10,12},{12... | collective-permute-start | bytes 786440 | tf_op jit(solution)/shard_map/ppermute | solution.py:123
  43.9 4.6 %collective-permute-start.3 = (f32[2,64,512]{2,1,0:T(8,128)}, f32[2,64,512]{2,1,0:T(8,128)}, u32[]{:S(2)}, u32[]{:S(2)}) collective-permute-start(f32[2,64,512]{2,1,0:T(8,128)} %get-tuple-element.33), channel_id=1, source_target_pairs={{0,6},{2,0},{4,2},{6,4},{1,7},{3,1},{5,3},{7,5},{8,14},{10,8},{12,... | collective-permute-start | bytes 786440 | tf_op jit(solution)/shard_map/ppermute | solution.py:123
  48.5 3.7 %shard_map.120 = (bf16[1024,512]{1,0:T(8,128)(2,1)}, bf16[512,512]{1,0:T(8,128)(2,1)}) custom-call(s32[4]{0:T(128)S(1)} %pad_add_fusion.at, bf16[1024,512]{1,0:T(8,128)(2,1)S(1)} %copy-done, bf16[512,512]{1,0:T(8,128)(2,1)S(1)} %copy-done.1, bf16[8,64,512]{2,1,0:T(8,128)(2,1)S(1)} %all-to-all-done.1.cot_mine, ...), custom_call_target="tpu_custom_call" | custom-call | bytes 3145728 | tf_op jit(solution)/shard_map/pallas_call | solution.py:186
  52.2 3.0 %collective-permute-done.2 = f32[2,64,512]{2,1,0:T(8,128)} collective-permute-done((f32[2,64,512]{2,1,0:T(8,128)}, f32[2,64,512]{2,1,0:T(8,128)}, u32[]{:S(2)}, u32[]{:S(2)}) %collective-permute-start.2) | collective-permute-done | bytes 262176 | tf_op jit(solution)/shard_map/ppermute | solution.py:123
  55.2 1.2 %add_add_fusion = f32[2,64,512]{2,1,0:T(8,128)S(1)} fusion(f32[2,64,512]{2,1,0:T(8,128)} %collective-permute-done.3, f32[2,64,512]{2,1,0:T(8,128)} %collective-permute-done.2, f32[2,64,512]{2,1,0:T(8,128)S(1)} %get-tuple-element.30, f32[2,64,512]{2,1,0:T(8,128)} %collective-permute-done.1), kind=kLoop, calls=%fused_computation | loop fusion | flops 196608 | bytes 1310720 | tf_op jit(solution)/shard_map/add | solution.py:197
  56.5 3.0 %collective-permute-start.5 = (f32[64,512]{1,0:T(8,128)S(1)}, f32[64,512]{1,0:T(8,128)S(1)}, u32[]{:S(2)}, u32[]{:S(2)}) collective-permute-start(f32[64,512]{1,0:T(8,128)S(1)} %get-tuple-element.47), channel_id=1, source_target_pairs={{0,8},{8,0},{1,9},{9,1},{2,10},{10,2},{3,11},{11,3},{4,12},{12,4},... | collective-permute-start | bytes 393224 | tf_op jit(solution)/shard_map/ppermute | solution.py:123
  59.5 4.5 %collective-permute-done.5.there = f32[64,512]{1,0:T(8,128)S(1)} collective-permute-done((f32[64,512]{1,0:T(8,128)S(1)}, f32[64,512]{1,0:T(8,128)S(1)}, u32[]{:S(2)}, u32[]{:S(2)}) %collective-permute-start.5) | collective-permute-done | bytes 131104 | tf_op jit(solution)/shard_map/ppermute | solution.py:123
  64.0 1.5 %shard_map.121 = (f32[16,512]{1,0:T(8,128)}, f32[4,16]{1,0:T(4,128)}, bf16[32,16,512]{2,1,0:T(8,128)(2,1)}, bf16[64,512]{1,0:T(8,128)(2,1)}) custom-call(bf16[32,32,512]{2,1,0:T(8,128)(2,1)S(1)} %all-to-all-done.got, bf16[32,16,512]{2,1,0:T(8,128)(2,1)S(1)} %bitcast.25, bf16[32,16,512]{2,1,0:T(8,128)(2,1)S(1)} %bitcast.26, ...), custom_call_target="tpu_custom_call" | custom-call | bytes 3145728 | tf_op jit(solution)/shard_map/pallas_call | solution.py:200
  (18 shorter events, 0.1 us)
Async XLA Ops:
  0.6 7.8 %copy-start = (bf16[1024,512]{1,0:T(8,128)(2,1)S(1)}, bf16[1024,512]{1,0:T(8,128)(2,1)}, u32[]{:S(2)}) copy-start(bf16[1024,512]{1,0:T(8,128)(2,1)} %tokens.1) | copy-start | bytes 3145732
  0.6 0.9 %copy-start.7 = (bf16[64,512]{1,0:T(8,128)(2,1)S(1)}, bf16[64,512]{1,0:T(8,128)(2,1)}, u32[]{:S(2)}) copy-start(bf16[64,512]{1,0:T(8,128)(2,1)} %rows.1) | copy-start | bytes 196612
  2.4 6.0 %copy-start.1 = (bf16[512,512]{1,0:T(8,128)(2,1)S(1)}, bf16[512,512]{1,0:T(8,128)(2,1)}, u32[]{:S(2)}) copy-start(bf16[512,512]{1,0:T(8,128)(2,1)} %weight.5) | copy-start | bytes 1572868
  2.4 14.5 %all-to-all-start.1 = ((bf16[8,64,512]{2,1,0:T(8,128)(2,1)}), bf16[8,64,512]{2,1,0:T(8,128)(2,1)S(1)}, u32[]{:S(2)}, u32[]{:S(2)}) async-start(bf16[8,64,512]{2,1,0:T(8,128)(2,1)} %shard_map.118), calls=%async_computation.1 | async-start | bytes 1048576 | tf_op jit(solution)/shard_map/all_to_all | solution.py:151
  8.3 0.8 %copy-start.8 = (f32[1,1,16,512]{3,2,1,0:T(8,128)S(1)}, f32[1,1,16,512]{3,2,1,0:T(8,128)}, u32[]{:S(2)}) copy-start(f32[1,1,16,512]{3,2,1,0:T(8,128)} %param.8) | copy-start | bytes 98308
  9.1 1.0 %copy-start.2 = (bf16[1,512,512]{2,1,0:T(8,128)(2,1)S(1)}, bf16[1,512,512]{2,1,0:T(8,128)(2,1)}, u32[]{:S(2)}) copy-start(bf16[1,512,512]{2,1,0:T(8,128)(2,1)} %param.6) | copy-start | bytes 1572868
  10.1 1.0 %copy-start.4 = (bf16[512,512]{1,0:T(8,128)(2,1)S(1)}, bf16[512,512]{1,0:T(8,128)(2,1)}, u32[]{:S(2)}) copy-start(bf16[512,512]{1,0:T(8,128)(2,1)} %stale.1) | copy-start | bytes 1572868
  13.4 1.0 %copy-start.6 = (bf16[32,32,512]{2,1,0:T(8,128)(2,1)}, bf16[32,32,512]{2,1,0:T(8,128)(2,1)S(1)}, u32[]{:S(2)}) copy-start(bf16[32,32,512]{2,1,0:T(8,128)(2,1)S(1)} %get-tuple-element.27) | copy-start | bytes 3145732
  14.4 18.4 %collective-permute-start = (f32[512,512]{1,0:T(8,128)}, f32[512,512]{1,0:T(8,128)}, u32[]{:S(2)}, u32[]{:S(2)}) collective-permute-start(f32[512,512]{1,0:T(8,128)} %get-tuple-element.28), channel_id=1, source_target_pairs={{0,1},{1,0},{2,3},{3,2},{4,5},{5,4},{6,7},{7,6},{8,9},{9,8},{10,11... | collective-permute-start | bytes 3145736 | tf_op jit(solution)/shard_map/ppermute | solution.py:123
  17.0 47.0 %all-to-all-start = ((bf16[32,32,512]{2,1,0:T(8,128)(2,1)}), bf16[32,32,512]{2,1,0:T(8,128)(2,1)S(1)}, u32[]{:S(2)}, u32[]{:S(2)}) async-start(bf16[32,32,512]{2,1,0:T(8,128)(2,1)} %copy-done.6), calls=%async_computation | async-start | bytes 2097152 | tf_op jit(solution)/shard_map/all_to_all | solution.py:173
  32.8 15.7 %collective-permute-start.4 = (bf16[8,64,512]{2,1,0:T(8,128)(2,1)S(1)}, bf16[8,64,512]{2,1,0:T(8,128)(2,1)}, u32[]{:S(2)}, u32[]{:S(2)}) collective-permute-start(bf16[8,64,512]{2,1,0:T(8,128)(2,1)S(1)} %all-to-all-done.1.cot_mine), channel_id=1, source_target_pairs={{0,1},{1,0},{2,3},{3,2},{4,5},{5,4},{6,7},{7,6},{8,9},{9,8},{10,11... | collective-permute-start | bytes 1572872 | tf_op jit(solution)/shard_map/ppermute | solution.py:123
  37.2 15.1 %collective-permute-start.1 = (f32[2,64,512]{2,1,0:T(8,128)}, f32[2,64,512]{2,1,0:T(8,128)}, u32[]{:S(2)}, u32[]{:S(2)}) collective-permute-start(f32[2,64,512]{2,1,0:T(8,128)} %get-tuple-element.31), channel_id=1, source_target_pairs={{0,4},{2,6},{4,0},{6,2},{1,5},{3,7},{5,1},{7,3},{8,12},{10,14},{12... | collective-permute-start | bytes 786440 | tf_op jit(solution)/shard_map/ppermute | solution.py:123
  41.4 13.8 %collective-permute-start.2 = (f32[2,64,512]{2,1,0:T(8,128)}, f32[2,64,512]{2,1,0:T(8,128)}, u32[]{:S(2)}, u32[]{:S(2)}) collective-permute-start(f32[2,64,512]{2,1,0:T(8,128)} %get-tuple-element.32), channel_id=1, source_target_pairs={{0,2},{2,4},{4,6},{6,0},{1,3},{3,5},{5,7},{7,1},{8,10},{10,12},{12... | collective-permute-start | bytes 786440 | tf_op jit(solution)/shard_map/ppermute | solution.py:123
  43.9 11.3 %collective-permute-start.3 = (f32[2,64,512]{2,1,0:T(8,128)}, f32[2,64,512]{2,1,0:T(8,128)}, u32[]{:S(2)}, u32[]{:S(2)}) collective-permute-start(f32[2,64,512]{2,1,0:T(8,128)} %get-tuple-element.33), channel_id=1, source_target_pairs={{0,6},{2,0},{4,2},{6,4},{1,7},{3,1},{5,3},{7,5},{8,14},{10,8},{12,... | collective-permute-start | bytes 786440 | tf_op jit(solution)/shard_map/ppermute | solution.py:123
  55.2 8.8 %copy-start.5 = (bf16[512,512]{1,0:T(8,128)(2,1)S(1)}, bf16[512,512]{1,0:T(8,128)(2,1)}, u32[]{:S(2)}) copy-start(bf16[512,512]{1,0:T(8,128)(2,1)} %stale.1) | copy-start | bytes 1572868
  56.5 7.5 %copy-start.3 = (bf16[1,512,512]{2,1,0:T(8,128)(2,1)S(1)}, bf16[1,512,512]{2,1,0:T(8,128)(2,1)}, u32[]{:S(2)}) copy-start(bf16[1,512,512]{2,1,0:T(8,128)(2,1)} %param.6) | copy-start | bytes 1572868
  56.5 7.5 %collective-permute-start.5 = (f32[64,512]{1,0:T(8,128)S(1)}, f32[64,512]{1,0:T(8,128)S(1)}, u32[]{:S(2)}, u32[]{:S(2)}) collective-permute-start(f32[64,512]{1,0:T(8,128)S(1)} %get-tuple-element.47), channel_id=1, source_target_pairs={{0,8},{8,0},{1,9},{9,1},{2,10},{10,2},{3,11},{11,3},{4,12},{12,4},... | collective-permute-start | bytes 393224 | tf_op jit(solution)/shard_map/ppermute | solution.py:123

commit v3 on v2

--- a/solution.py
+++ b/solution.py
@@ -99,7 +99,7 @@
     ).astype(BF16)
 
 
-def tail_kernel(got, grads, stale, weight, here, there, codes, scales, new_weight, keys):
+def tail_kernel(got, grads, stale, weight, codes, scales, new_weight):
     replicas, twice, width = got.shape
     owned = twice // 2
     total = jnp.sum(got[:, :owned, :].astype(F32), axis=0)
@@ -115,7 +115,6 @@
         scales[b:b + 1, :] = jnp.sum(jnp.where(diagonal, scale, 0.0), axis=0, keepdims=True)
     change = got[:, owned:, :].astype(F32) + (grads[...].astype(F32) - stale[...].astype(F32)) / replicas
     new_weight[...] = (weight[...].astype(F32) - OUTER_RATE * change).astype(BF16)
-    keys[...] = (here[...] + there[...]).astype(BF16)
 
 
 def shift(value, axis, k):
@@ -197,19 +196,20 @@
     acc = kept + from_x[0] + from_x[1] + from_x[2]
     there = shift(pick(acc, 1 - yl_at, 0), "yl", 1)
 
-    codes, scales, new_weight, keys = call(
+    codes, scales, new_weight = call(
         tail_kernel,
-        [VMEM] * 6,
+        [VMEM] * 4,
         [
             ((owned, width), F32, VMEM),
             ((nblocks, owned), F32, VMEM),
             ((replicas, owned, width), BF16, VMEM),
-            ((mine, width), BF16, VMEM),
         ],
         12 * block,
         0,
         limit=12 * MIB,
-    )(got, grads, stale_avg.reshape(grads.shape), weight.reshape(grads.shape), pick(acc, yl_at, 0), there)
+    )(got, grads, stale_avg.reshape(grads.shape), weight.reshape(grads.shape))
+    codes, there = lax.optimization_barrier((codes, there))
+    keys = (pick(acc, yl_at, 0) + there).astype(BF16)
     return (
         codes[None, None],
         scales.T[None, None],

time: 66.2 us -> 66.3 us (level)
  the two profiles are of different devices: /device:TPU:40 before, /device:TPU:72 now
where the time goes in v3:
time: 66.3 us; the launch traced here: 65.5 us
  starting transfers between devices  38.4 us (58%)
  Pallas kernels  10.7 us (16%)
  waiting for transfers between devices  8.98 us (14%)
  local copies, waits for them, and re-layouts  4.71 us (7%)
  other arithmetic  2 us (3%)
  between operations  0.79 us (1%)
    ppermute x6, starting transfers between devices, shift(): return lax.ppermute(value, axis, [(i, (i + k) % n) for i in range(n)])  18 us
    all_to_all x1, starting transfers between devices, body(): got = lax.all_to_all(sent, REPLICA, 0, 0)  14.5 us
    all_to_all x1, starting transfers between devices, body(): cot_mine = lax.all_to_all(copies, CHIPS, 0, 0)  5.9 us
    all_to_all x1, waiting for transfers between devices, body(): got = lax.all_to_all(sent, REPLICA, 0, 0)  5.38 us
    unnamed x18, local copies, waits for them, and re-layouts  4.69 us
    pallas_call x1, Pallas kernels, body(): call(grads_kernel, [SMEM, VMEM, VMEM, HBM, HBM], [(tokens.shape, BF16, VM...  3.72 us
    ppermute x6, waiting for transfers between devices, shift(): return lax.ppermute(value, axis, [(i, (i + k) % n) for i in range(n)])  2.96 us
    pallas_call x1, Pallas kernels, body(): call(own_kernel, [SMEM, VMEM, VMEM, VMEM], [((runs, mine, width), F32, VM...  2.42 us
  transfers between devices with their start and end apart: 8, of which 3 were waited for; matrix products, arithmetic and copies ran while one was open for 2% of the time, Pallas kernels for 15%

profile of v3, /device:TPU:72, one launch (start us, length us, event | category | flops | bytes accessed | tf_op | source)
XLA Modules:
  0.0 65.5 jit_solution(10247458186090550399)
XLA Ops:
  0.7 0.9 %copy-done.7 = bf16[64,512]{1,0:T(8,128)(2,1)S(1)} copy-done((bf16[64,512]{1,0:T(8,128)(2,1)S(1)}, bf16[64,512]{1,0:T(8,128)(2,1)}, u32[]{:S(2)}) %copy-start.7) | copy-done | bytes 65560
  1.6 0.8 %shard_map.119 = bf16[8,64,512]{2,1,0:T(8,128)(2,1)} custom-call(bf16[64,512]{1,0:T(8,128)(2,1)S(1)} %copy-done.7), custom_call_target="tpu_custom_call" | custom-call | bytes 1048576 | tf_op jit(solution)/shard_map/pallas_call | solution.py:142
  2.4 5.9 %all-to-all-start.1 = ((bf16[8,64,512]{2,1,0:T(8,128)(2,1)}), bf16[8,64,512]{2,1,0:T(8,128)(2,1)S(1)}, u32[]{:S(2)}, u32[]{:S(2)}) async-start(bf16[8,64,512]{2,1,0:T(8,128)(2,1)} %shard_map.119), calls=%async_computation.1 | async-start | bytes 1048576 | tf_op jit(solution)/shard_map/all_to_all | solution.py:150
  8.3 0.1 pad_add_fusion.at
  8.4 0.7 %copy-done.8 = f32[1,1,16,512]{3,2,1,0:T(8,128)S(1)} copy-done((f32[1,1,16,512]{3,2,1,0:T(8,128)S(1)}, f32[1,1,16,512]{3,2,1,0:T(8,128)}, u32[]{:S(2)}) %copy-start.8) | copy-done | bytes 32792
  9.1 1.0 %copy-done.2 = bf16[1,512,512]{2,1,0:T(8,128)(2,1)S(1)} copy-done((bf16[1,512,512]{2,1,0:T(8,128)(2,1)S(1)}, bf16[1,512,512]{2,1,0:T(8,128)(2,1)}, u32[]{:S(2)}) %copy-start.2) | copy-done | bytes 524312
  10.1 1.0 %copy-done.4 = bf16[512,512]{1,0:T(8,128)(2,1)S(1)} copy-done((bf16[512,512]{1,0:T(8,128)(2,1)S(1)}, bf16[512,512]{1,0:T(8,128)(2,1)}, u32[]{:S(2)}) %copy-start.4) | copy-done | bytes 524312
  11.2 2.2 %shard_map.117 = (bf16[32,32,512]{2,1,0:T(8,128)(2,1)S(1)}, f32[16,512]{1,0:T(8,128)}, f32[512,512]{1,0:T(8,128)}) custom-call(s32[4]{0:T(128)S(1)} %pad_add_fusion.at, bf16[32,16,512]{2,1,0:T(8,128)(2,1)S(1)} %bitcast.26, bf16[512,512]{1,0:T(8,128)(2,1)S(1)} %copy-done.4, f32[16,512]{1,0:T(8,128)S(1)} %bitcast.29, bf16[8,2,64,512]{3,2,1,0:T(8,128)(2,1)S(1)} %bitcast.23, ...), custom_call_target="tpu_custom_call" | custom-call | bytes 3145728 | tf_op jit(solution)/shard_map/pallas_call | solution.py:154
  13.4 1.0 %copy-done.6 = bf16[32,32,512]{2,1,0:T(8,128)(2,1)} copy-done((bf16[32,32,512]{2,1,0:T(8,128)(2,1)}, bf16[32,32,512]{2,1,0:T(8,128)(2,1)S(1)}, u32[]{:S(2)}) %copy-start.6) | copy-done | bytes 1048600
  14.4 1.9 %collective-permute-start = (f32[512,512]{1,0:T(8,128)}, f32[512,512]{1,0:T(8,128)}, u32[]{:S(2)}, u32[]{:S(2)}) collective-permute-start(f32[512,512]{1,0:T(8,128)} %get-tuple-element.30), channel_id=1, source_target_pairs={{0,1},{1,0},{2,3},{3,2},{4,5},{5,4},{6,7},{7,6},{8,9},{9,8},{10,11... | collective-permute-start | bytes 3145736 | tf_op jit(solution)/shard_map/ppermute | solution.py:122
  16.3 0.6 all-to-all-done.1.cot_mine
  17.0 14.5 %all-to-all-start = ((bf16[32,32,512]{2,1,0:T(8,128)(2,1)}), bf16[32,32,512]{2,1,0:T(8,128)(2,1)S(1)}, u32[]{:S(2)}, u32[]{:S(2)}) async-start(bf16[32,32,512]{2,1,0:T(8,128)(2,1)} %copy-done.6), calls=%async_computation | async-start | bytes 2097152 | tf_op jit(solution)/shard_map/all_to_all | solution.py:172
  31.5 1.9 %collective-permute-start.4 = (bf16[8,64,512]{2,1,0:T(8,128)(2,1)S(1)}, bf16[8,64,512]{2,1,0:T(8,128)(2,1)}, u32[]{:S(2)}, u32[]{:S(2)}) collective-permute-start(bf16[8,64,512]{2,1,0:T(8,128)(2,1)S(1)} %all-to-all-done.1.cot_mine), channel_id=1, source_target_pairs={{0,1},{1,0},{2,3},{3,2},{4,5},{5,4},{6,7},{7,6},{8,9},{9,8},{10,11... | collective-permute-start | bytes 1572872 | tf_op jit(solution)/shard_map/ppermute | solution.py:122
  33.4 2.4 %shard_map.120 = (f32[2,64,512]{2,1,0:T(8,128)S(1)}, f32[2,64,512]{2,1,0:T(8,128)}, f32[2,64,512]{2,1,0:T(8,128)}, f32[2,64,512]{2,1,0:T(8,128)}) custom-call(s32[4]{0:T(128)S(1)} %pad_add_fusion.at, bf16[8,2,64,512]{3,2,1,0:T(8,128)(2,1)S(1)} %bitcast.24, bf16[512,512]{1,0:T(8,128)(2,1)S(1)} %copy-done.1, f32[8,64,512]{2,1,0:T(8,128)} %bitcast.9.arrived), custom_call_target="tpu_custom_call" | custom-call | bytes 2621440 | tf_op jit(solution)/shard_map/pallas_call | solution.py:175
  35.8 4.3 %collective-permute-start.1 = (f32[2,64,512]{2,1,0:T(8,128)}, f32[2,64,512]{2,1,0:T(8,128)}, u32[]{:S(2)}, u32[]{:S(2)}) collective-permute-start(f32[2,64,512]{2,1,0:T(8,128)} %get-tuple-element.33), channel_id=1, source_target_pairs={{0,4},{2,6},{4,0},{6,2},{1,5},{3,7},{5,1},{7,3},{8,12},{10,14},{12... | collective-permute-start | bytes 786440 | tf_op jit(solution)/shard_map/ppermute | solution.py:122
  40.1 2.5 %collective-permute-start.2 = (f32[2,64,512]{2,1,0:T(8,128)}, f32[2,64,512]{2,1,0:T(8,128)}, u32[]{:S(2)}, u32[]{:S(2)}) collective-permute-start(f32[2,64,512]{2,1,0:T(8,128)} %get-tuple-element.34), channel_id=1, source_target_pairs={{0,2},{2,4},{4,6},{6,0},{1,3},{3,5},{5,7},{7,1},{8,10},{10,12},{12... | collective-permute-start | bytes 786440 | tf_op jit(solution)/shard_map/ppermute | solution.py:122
  42.6 4.6 %collective-permute-start.3 = (f32[2,64,512]{2,1,0:T(8,128)}, f32[2,64,512]{2,1,0:T(8,128)}, u32[]{:S(2)}, u32[]{:S(2)}) collective-permute-start(f32[2,64,512]{2,1,0:T(8,128)} %get-tuple-element.35), channel_id=1, source_target_pairs={{0,6},{2,0},{4,2},{6,4},{1,7},{3,1},{5,3},{7,5},{8,14},{10,8},{12,... | collective-permute-start | bytes 786440 | tf_op jit(solution)/shard_map/ppermute | solution.py:122
  47.2 3.7 %shard_map.121 = (bf16[1024,512]{1,0:T(8,128)(2,1)}, bf16[512,512]{1,0:T(8,128)(2,1)}) custom-call(s32[4]{0:T(128)S(1)} %pad_add_fusion.at, bf16[1024,512]{1,0:T(8,128)(2,1)S(1)} %copy-done, bf16[512,512]{1,0:T(8,128)(2,1)S(1)} %copy-done.1, bf16[8,64,512]{2,1,0:T(8,128)(2,1)S(1)} %all-to-all-done.1.cot_mine, ...), custom_call_target="tpu_custom_call" | custom-call | bytes 3145728 | tf_op jit(solution)/shard_map/pallas_call | solution.py:185
  50.9 3.0 %collective-permute-done.2 = f32[2,64,512]{2,1,0:T(8,128)} collective-permute-done((f32[2,64,512]{2,1,0:T(8,128)}, f32[2,64,512]{2,1,0:T(8,128)}, u32[]{:S(2)}, u32[]{:S(2)}) %collective-permute-start.2) | collective-permute-done | bytes 262176 | tf_op jit(solution)/shard_map/ppermute | solution.py:122
  53.9 1.3 %add_add_fusion = f32[2,64,512]{2,1,0:T(8,128)S(1)} fusion(f32[2,64,512]{2,1,0:T(8,128)} %collective-permute-done.3, f32[2,64,512]{2,1,0:T(8,128)} %collective-permute-done.2, f32[2,64,512]{2,1,0:T(8,128)S(1)} %get-tuple-element.32, f32[2,64,512]{2,1,0:T(8,128)} %collective-permute-done.1), kind=kLoop, calls=%fused_computation | loop fusion | flops 196608 | bytes 1310720 | tf_op jit(solution)/shard_map/add | solution.py:196
  55.2 2.9 %collective-permute-start.5 = (f32[64,512]{1,0:T(8,128)S(1)}, f32[64,512]{1,0:T(8,128)S(1)}, u32[]{:S(2)}, u32[]{:S(2)}) collective-permute-start(f32[64,512]{1,0:T(8,128)S(1)} %dynamic-slice_bitcast_fusion), channel_id=1, source_target_pairs={{0,8},{8,0},{1,9},{9,1},{2,10},{10,2},{3,11},{11,3},{4,12},{12,4},... | collective-permute-start | bytes 393224 | tf_op jit(solution)/shard_map/ppermute | solution.py:122
  58.0 5.4 %all-to-all-done.got = bf16[32,32,512]{2,1,0:T(8,128)(2,1)S(1)} async-done(((bf16[32,32,512]{2,1,0:T(8,128)(2,1)}), bf16[32,32,512]{2,1,0:T(8,128)(2,1)S(1)}, u32[]{:S(2)}, u32[]{:S(2)}) %all-to-all-start) | async-done | bytes 1048608 | tf_op jit(solution)/shard_map/all_to_all | solution.py:172
  63.4 1.5 %shard_map.118 = (f32[16,512]{1,0:T(8,128)}, f32[4,16]{1,0:T(4,128)}, bf16[32,16,512]{2,1,0:T(8,128)(2,1)}) custom-call(bf16[32,32,512]{2,1,0:T(8,128)(2,1)S(1)} %all-to-all-done.got, bf16[32,16,512]{2,1,0:T(8,128)(2,1)S(1)} %bitcast.27, bf16[32,16,512]{2,1,0:T(8,128)(2,1)S(1)} %bitcast.28, bf16[32,16,512]{2,1,0:T(8,128)(2,1)S(1)} %bitcast.25), custom_call_target="tpu_custom_call" | custom-call | bytes 3145728 | tf_op jit(solution)/shard_map/pallas_call | solution.py:199
  64.9 0.6 fusion
  (19 shorter events, 0.1 us)
Async XLA Ops:
  0.6 7.8 %copy-start = (bf16[1024,512]{1,0:T(8,128)(2,1)S(1)}, bf16[1024,512]{1,0:T(8,128)(2,1)}, u32[]{:S(2)}) copy-start(bf16[1024,512]{1,0:T(8,128)(2,1)} %tokens.1) | copy-start | bytes 3145732
  0.6 0.9 %copy-start.7 = (bf16[64,512]{1,0:T(8,128)(2,1)S(1)}, bf16[64,512]{1,0:T(8,128)(2,1)}, u32[]{:S(2)}) copy-start(bf16[64,512]{1,0:T(8,128)(2,1)} %rows.1) | copy-start | bytes 196612
  2.4 6.0 %copy-start.1 = (bf16[512,512]{1,0:T(8,128)(2,1)S(1)}, bf16[512,512]{1,0:T(8,128)(2,1)}, u32[]{:S(2)}) copy-start(bf16[512,512]{1,0:T(8,128)(2,1)} %weight.5) | copy-start | bytes 1572868
  2.4 14.5 %all-to-all-start.1 = ((bf16[8,64,512]{2,1,0:T(8,128)(2,1)}), bf16[8,64,512]{2,1,0:T(8,128)(2,1)S(1)}, u32[]{:S(2)}, u32[]{:S(2)}) async-start(bf16[8,64,512]{2,1,0:T(8,128)(2,1)} %shard_map.119), calls=%async_computation.1 | async-start | bytes 1048576 | tf_op jit(solution)/shard_map/all_to_all | solution.py:150
  8.3 0.8 %copy-start.8 = (f32[1,1,16,512]{3,2,1,0:T(8,128)S(1)}, f32[1,1,16,512]{3,2,1,0:T(8,128)}, u32[]{:S(2)}) copy-start(f32[1,1,16,512]{3,2,1,0:T(8,128)} %param.8) | copy-start | bytes 98308
  9.1 1.0 %copy-start.2 = (bf16[1,512,512]{2,1,0:T(8,128)(2,1)S(1)}, bf16[1,512,512]{2,1,0:T(8,128)(2,1)}, u32[]{:S(2)}) copy-start(bf16[1,512,512]{2,1,0:T(8,128)(2,1)} %param.6) | copy-start | bytes 1572868
  10.1 1.0 %copy-start.4 = (bf16[512,512]{1,0:T(8,128)(2,1)S(1)}, bf16[512,512]{1,0:T(8,128)(2,1)}, u32[]{:S(2)}) copy-start(bf16[512,512]{1,0:T(8,128)(2,1)} %stale.1) | copy-start | bytes 1572868
  13.4 1.0 %copy-start.6 = (bf16[32,32,512]{2,1,0:T(8,128)(2,1)}, bf16[32,32,512]{2,1,0:T(8,128)(2,1)S(1)}, u32[]{:S(2)}) copy-start(bf16[32,32,512]{2,1,0:T(8,128)(2,1)S(1)} %get-tuple-element.28) | copy-start | bytes 3145732
  14.4 17.1 %collective-permute-start = (f32[512,512]{1,0:T(8,128)}, f32[512,512]{1,0:T(8,128)}, u32[]{:S(2)}, u32[]{:S(2)}) collective-permute-start(f32[512,512]{1,0:T(8,128)} %get-tuple-element.30), channel_id=1, source_target_pairs={{0,1},{1,0},{2,3},{3,2},{4,5},{5,4},{6,7},{7,6},{8,9},{9,8},{10,11... | collective-permute-start | bytes 3145736 | tf_op jit(solution)/shard_map/ppermute | solution.py:122
  17.0 46.4 %all-to-all-start = ((bf16[32,32,512]{2,1,0:T(8,128)(2,1)}), bf16[32,32,512]{2,1,0:T(8,128)(2,1)S(1)}, u32[]{:S(2)}, u32[]{:S(2)}) async-start(bf16[32,32,512]{2,1,0:T(8,128)(2,1)} %copy-done.6), calls=%async_computation | async-start | bytes 2097152 | tf_op jit(solution)/shard_map/all_to_all | solution.py:172
  31.5 15.7 %collective-permute-start.4 = (bf16[8,64,512]{2,1,0:T(8,128)(2,1)S(1)}, bf16[8,64,512]{2,1,0:T(8,128)(2,1)}, u32[]{:S(2)}, u32[]{:S(2)}) collective-permute-start(bf16[8,64,512]{2,1,0:T(8,128)(2,1)S(1)} %all-to-all-done.1.cot_mine), channel_id=1, source_target_pairs={{0,1},{1,0},{2,3},{3,2},{4,5},{5,4},{6,7},{7,6},{8,9},{9,8},{10,11... | collective-permute-start | bytes 1572872 | tf_op jit(solution)/shard_map/ppermute | solution.py:122
  35.8 15.1 %collective-permute-start.1 = (f32[2,64,512]{2,1,0:T(8,128)}, f32[2,64,512]{2,1,0:T(8,128)}, u32[]{:S(2)}, u32[]{:S(2)}) collective-permute-start(f32[2,64,512]{2,1,0:T(8,128)} %get-tuple-element.33), channel_id=1, source_target_pairs={{0,4},{2,6},{4,0},{6,2},{1,5},{3,7},{5,1},{7,3},{8,12},{10,14},{12... | collective-permute-start | bytes 786440 | tf_op jit(solution)/shard_map/ppermute | solution.py:122
  40.1 13.8 %collective-permute-start.2 = (f32[2,64,512]{2,1,0:T(8,128)}, f32[2,64,512]{2,1,0:T(8,128)}, u32[]{:S(2)}, u32[]{:S(2)}) collective-permute-start(f32[2,64,512]{2,1,0:T(8,128)} %get-tuple-element.34), channel_id=1, source_target_pairs={{0,2},{2,4},{4,6},{6,0},{1,3},{3,5},{5,7},{7,1},{8,10},{10,12},{12... | collective-permute-start | bytes 786440 | tf_op jit(solution)/shard_map/ppermute | solution.py:122
  42.6 11.3 %collective-permute-start.3 = (f32[2,64,512]{2,1,0:T(8,128)}, f32[2,64,512]{2,1,0:T(8,128)}, u32[]{:S(2)}, u32[]{:S(2)}) collective-permute-start(f32[2,64,512]{2,1,0:T(8,128)} %get-tuple-element.35), channel_id=1, source_target_pairs={{0,6},{2,0},{4,2},{6,4},{1,7},{3,1},{5,3},{7,5},{8,14},{10,8},{12,... | collective-permute-start | bytes 786440 | tf_op jit(solution)/shard_map/ppermute | solution.py:122
  53.8 9.6 %copy-start.3 = (bf16[1,512,512]{2,1,0:T(8,128)(2,1)S(1)}, bf16[1,512,512]{2,1,0:T(8,128)(2,1)}, u32[]{:S(2)}) copy-start(bf16[1,512,512]{2,1,0:T(8,128)(2,1)} %param.6) | copy-start | bytes 1572868
  53.9 9.6 %copy-start.5 = (bf16[512,512]{1,0:T(8,128)(2,1)S(1)}, bf16[512,512]{1,0:T(8,128)(2,1)}, u32[]{:S(2)}) copy-start(bf16[512,512]{1,0:T(8,128)(2,1)} %stale.1) | copy-start | bytes 1572868
  55.2 9.7 %collective-permute-start.5 = (f32[64,512]{1,0:T(8,128)S(1)}, f32[64,512]{1,0:T(8,128)S(1)}, u32[]{:S(2)}, u32[]{:S(2)}) collective-permute-start(f32[64,512]{1,0:T(8,128)S(1)} %dynamic-slice_bitcast_fusion), channel_id=1, source_target_pairs={{0,8},{8,0},{1,9},{9,1},{2,10},{10,2},{3,11},{11,3},{4,12},{12,4},... | collective-permute-start | bytes 393224 | tf_op jit(solution)/shard_map/ppermute | solution.py:122

commit v4 on v2

--- a/solution.py
+++ b/solution.py
@@ -182,6 +182,7 @@
     )(at, grouped, weight, arrived)
     from_x = [shift(pieces[k - 1], "x", k) for k in (2, 1, 3)]
 
+    kept, cot_mine = lax.optimization_barrier((kept, cot_mine))
     cot_theirs = shift(cot_mine, "core", 1)
     grad_tokens, grad_weight = call(
         grads_kernel,

time: 66.2 us -> 66.2 us (level)
  no operation moved by 1% of the time
where the time goes in v4:
time: 66.2 us; the launch traced here: 65.5 us
  starting transfers between devices  39.9 us (60%)
  Pallas kernels  10.7 us (16%)
  waiting for transfers between devices  8.08 us (12%)
  local copies, waits for them, and re-layouts  4.71 us (7%)
  other arithmetic  1.33 us (2%)
  between operations  0.8 us (1%)
    ppermute x6, starting transfers between devices, shift(): return lax.ppermute(value, axis, [(i, (i + k) % n) for i in range(n)])  18.1 us
    all_to_all x1, starting transfers between devices, body(): got = lax.all_to_all(sent, REPLICA, 0, 0)  15.8 us
    ppermute x6, waiting for transfers between devices, shift(): return lax.ppermute(value, axis, [(i, (i + k) % n) for i in range(n)])  7.43 us
    all_to_all x1, starting transfers between devices, body(): cot_mine = lax.all_to_all(copies, CHIPS, 0, 0)  5.9 us
    unnamed x18, local copies, waits for them, and re-layouts  4.69 us
    pallas_call x1, Pallas kernels, body(): call(grads_kernel, [SMEM, VMEM, VMEM, HBM, HBM], [(tokens.shape, BF16, VM...  3.72 us
    pallas_call x1, Pallas kernels, body(): call(own_kernel, [SMEM, VMEM, VMEM, VMEM], [((runs, mine, width), F32, VM...  2.42 us
    pallas_call x1, Pallas kernels, body(): call(front_kernel, [SMEM, HBM, HBM, VMEM, HBM, VMEM], [((replicas, 2 * ow...  2.22 us
  transfers between devices with their start and end apart: 8, of which 3 were waited for; matrix products, arithmetic and copies ran while one was open for 2% of the time, Pallas kernels for 13%

profile of v4, /device:TPU:40, one launch (start us, length us, event | category | flops | bytes accessed | tf_op | source)
XLA Modules:
  0.0 65.5 jit_solution(16760402731093083482)
XLA Ops:
  0.7 0.9 %copy-done.7 = bf16[64,512]{1,0:T(8,128)(2,1)S(1)} copy-done((bf16[64,512]{1,0:T(8,128)(2,1)S(1)}, bf16[64,512]{1,0:T(8,128)(2,1)}, u32[]{:S(2)}) %copy-start.7) | copy-done | bytes 65560
  1.6 0.8 %shard_map.118 = bf16[8,64,512]{2,1,0:T(8,128)(2,1)} custom-call(bf16[64,512]{1,0:T(8,128)(2,1)S(1)} %copy-done.7), custom_call_target="tpu_custom_call" | custom-call | bytes 1048576 | tf_op jit(solution)/shard_map/pallas_call | solution.py:143
  2.4 5.9 %all-to-all-start.1 = ((bf16[8,64,512]{2,1,0:T(8,128)(2,1)}), bf16[8,64,512]{2,1,0:T(8,128)(2,1)S(1)}, u32[]{:S(2)}, u32[]{:S(2)}) async-start(bf16[8,64,512]{2,1,0:T(8,128)(2,1)} %shard_map.118), calls=%async_computation.1 | async-start | bytes 1048576 | tf_op jit(solution)/shard_map/all_to_all | solution.py:151
  8.3 0.1 pad_add_fusion.at
  8.4 0.7 %copy-done.8 = f32[1,1,16,512]{3,2,1,0:T(8,128)S(1)} copy-done((f32[1,1,16,512]{3,2,1,0:T(8,128)S(1)}, f32[1,1,16,512]{3,2,1,0:T(8,128)}, u32[]{:S(2)}) %copy-start.8) | copy-done | bytes 32792
  9.1 1.0 %copy-done.2 = bf16[1,512,512]{2,1,0:T(8,128)(2,1)S(1)} copy-done((bf16[1,512,512]{2,1,0:T(8,128)(2,1)S(1)}, bf16[1,512,512]{2,1,0:T(8,128)(2,1)}, u32[]{:S(2)}) %copy-start.2) | copy-done | bytes 524312
  10.1 1.0 %copy-done.4 = bf16[512,512]{1,0:T(8,128)(2,1)S(1)} copy-done((bf16[512,512]{1,0:T(8,128)(2,1)S(1)}, bf16[512,512]{1,0:T(8,128)(2,1)}, u32[]{:S(2)}) %copy-start.4) | copy-done | bytes 524312
  11.2 2.2 %shard_map.117 = (bf16[32,32,512]{2,1,0:T(8,128)(2,1)S(1)}, f32[16,512]{1,0:T(8,128)}, f32[512,512]{1,0:T(8,128)}) custom-call(s32[4]{0:T(128)S(1)} %pad_add_fusion.at, bf16[32,16,512]{2,1,0:T(8,128)(2,1)S(1)} %bitcast.24, bf16[512,512]{1,0:T(8,128)(2,1)S(1)} %copy-done.4, f32[16,512]{1,0:T(8,128)S(1)} %bitcast.27, bf16[8,2,64,512]{3,2,1,0:T(8,128)(2,1)S(1)} %bitcast.21, ...), custom_call_target="tpu_custom_call" | custom-call | bytes 3145728 | tf_op jit(solution)/shard_map/pallas_call | solution.py:155
  13.4 1.0 %copy-done.6 = bf16[32,32,512]{2,1,0:T(8,128)(2,1)} copy-done((bf16[32,32,512]{2,1,0:T(8,128)(2,1)}, bf16[32,32,512]{2,1,0:T(8,128)(2,1)S(1)}, u32[]{:S(2)}) %copy-start.6) | copy-done | bytes 1048600
  14.4 1.9 %collective-permute-start = (f32[512,512]{1,0:T(8,128)}, f32[512,512]{1,0:T(8,128)}, u32[]{:S(2)}, u32[]{:S(2)}) collective-permute-start(f32[512,512]{1,0:T(8,128)} %get-tuple-element.30), channel_id=1, source_target_pairs={{0,1},{1,0},{2,3},{3,2},{4,5},{5,4},{6,7},{7,6},{8,9},{9,8},{10,11... | collective-permute-start | bytes 3145736 | tf_op jit(solution)/shard_map/ppermute | solution.py:123
  16.3 0.6 all-to-all-done.1.cot_mine
  17.0 15.8 %all-to-all-start = ((bf16[32,32,512]{2,1,0:T(8,128)(2,1)}), bf16[32,32,512]{2,1,0:T(8,128)(2,1)S(1)}, u32[]{:S(2)}, u32[]{:S(2)}) async-start(bf16[32,32,512]{2,1,0:T(8,128)(2,1)} %copy-done.6), calls=%async_computation | async-start | bytes 2097152 | tf_op jit(solution)/shard_map/all_to_all | solution.py:173
  32.8 2.4 %shard_map.119 = (f32[2,64,512]{2,1,0:T(8,128)S(1)}, f32[2,64,512]{2,1,0:T(8,128)}, f32[2,64,512]{2,1,0:T(8,128)}, f32[2,64,512]{2,1,0:T(8,128)}) custom-call(s32[4]{0:T(128)S(1)} %pad_add_fusion.at, bf16[8,2,64,512]{3,2,1,0:T(8,128)(2,1)S(1)} %bitcast.22, bf16[512,512]{1,0:T(8,128)(2,1)S(1)} %copy-done.1, f32[8,64,512]{2,1,0:T(8,128)} %bitcast.9.arrived), custom_call_target="tpu_custom_call" | custom-call | bytes 2621440 | tf_op jit(solution)/shard_map/pallas_call | solution.py:176
  35.2 1.9 %collective-permute-start.4 = (bf16[8,64,512]{2,1,0:T(8,128)(2,1)S(1)}, bf16[8,64,512]{2,1,0:T(8,128)(2,1)}, u32[]{:S(2)}, u32[]{:S(2)}) collective-permute-start(bf16[8,64,512]{2,1,0:T(8,128)(2,1)S(1)} %all-to-all-done.1.cot_mine), channel_id=1, source_target_pairs={{0,1},{1,0},{2,3},{3,2},{4,5},{5,4},{6,7},{7,6},{8,9},{9,8},{10,11... | collective-permute-start | bytes 1572872 | tf_op jit(solution)/shard_map/ppermute | solution.py:123
  37.2 4.3 %collective-permute-start.1 = (f32[2,64,512]{2,1,0:T(8,128)}, f32[2,64,512]{2,1,0:T(8,128)}, u32[]{:S(2)}, u32[]{:S(2)}) collective-permute-start(f32[2,64,512]{2,1,0:T(8,128)} %get-tuple-element.35), channel_id=1, source_target_pairs={{0,4},{2,6},{4,0},{6,2},{1,5},{3,7},{5,1},{7,3},{8,12},{10,14},{12... | collective-permute-start | bytes 786440 | tf_op jit(solution)/shard_map/ppermute | solution.py:123
  41.4 2.5 %collective-permute-start.2 = (f32[2,64,512]{2,1,0:T(8,128)}, f32[2,64,512]{2,1,0:T(8,128)}, u32[]{:S(2)}, u32[]{:S(2)}) collective-permute-start(f32[2,64,512]{2,1,0:T(8,128)} %get-tuple-element.36), channel_id=1, source_target_pairs={{0,2},{2,4},{4,6},{6,0},{1,3},{3,5},{5,7},{7,1},{8,10},{10,12},{12... | collective-permute-start | bytes 786440 | tf_op jit(solution)/shard_map/ppermute | solution.py:123
  43.9 4.6 %collective-permute-start.3 = (f32[2,64,512]{2,1,0:T(8,128)}, f32[2,64,512]{2,1,0:T(8,128)}, u32[]{:S(2)}, u32[]{:S(2)}) collective-permute-start(f32[2,64,512]{2,1,0:T(8,128)} %get-tuple-element.37), channel_id=1, source_target_pairs={{0,6},{2,0},{4,2},{6,4},{1,7},{3,1},{5,3},{7,5},{8,14},{10,8},{12,... | collective-permute-start | bytes 786440 | tf_op jit(solution)/shard_map/ppermute | solution.py:123
  48.5 3.7 %shard_map.120 = (bf16[1024,512]{1,0:T(8,128)(2,1)}, bf16[512,512]{1,0:T(8,128)(2,1)}) custom-call(s32[4]{0:T(128)S(1)} %pad_add_fusion.at, bf16[1024,512]{1,0:T(8,128)(2,1)S(1)} %copy-done, bf16[512,512]{1,0:T(8,128)(2,1)S(1)} %copy-done.1, bf16[8,64,512]{2,1,0:T(8,128)(2,1)S(1)} %all-to-all-done.1.cot_mine, ...), custom_call_target="tpu_custom_call" | custom-call | bytes 3145728 | tf_op jit(solution)/shard_map/pallas_call | solution.py:187
  52.2 3.0 %collective-permute-done.2 = f32[2,64,512]{2,1,0:T(8,128)} collective-permute-done((f32[2,64,512]{2,1,0:T(8,128)}, f32[2,64,512]{2,1,0:T(8,128)}, u32[]{:S(2)}, u32[]{:S(2)}) %collective-permute-start.2) | collective-permute-done | bytes 262176 | tf_op jit(solution)/shard_map/ppermute | solution.py:123
  55.2 1.2 %add_add_fusion = f32[2,64,512]{2,1,0:T(8,128)S(1)} fusion(f32[2,64,512]{2,1,0:T(8,128)} %collective-permute-done.3, f32[2,64,512]{2,1,0:T(8,128)} %collective-permute-done.2, f32[2,64,512]{2,1,0:T(8,128)S(1)} %get-tuple-element.34, f32[2,64,512]{2,1,0:T(8,128)} %collective-permute-done.1), kind=kLoop, calls=%fused_computation | loop fusion | flops 196608 | bytes 1310720 | tf_op jit(solution)/shard_map/add | solution.py:198
  56.5 0.0 copy-start.3
  56.5 3.0 %collective-permute-start.5 = (f32[64,512]{1,0:T(8,128)S(1)}, f32[64,512]{1,0:T(8,128)S(1)}, u32[]{:S(2)}, u32[]{:S(2)}) collective-permute-start(f32[64,512]{1,0:T(8,128)S(1)} %get-tuple-element.51), channel_id=1, source_target_pairs={{0,8},{8,0},{1,9},{9,1},{2,10},{10,2},{3,11},{11,3},{4,12},{12,4},... | collective-permute-start | bytes 393224 | tf_op jit(solution)/shard_map/ppermute | solution.py:123
  59.5 4.5 %collective-permute-done.5.there = f32[64,512]{1,0:T(8,128)S(1)} collective-permute-done((f32[64,512]{1,0:T(8,128)S(1)}, f32[64,512]{1,0:T(8,128)S(1)}, u32[]{:S(2)}, u32[]{:S(2)}) %collective-permute-start.5) | collective-permute-done | bytes 131104 | tf_op jit(solution)/shard_map/ppermute | solution.py:123
  64.0 1.5 %shard_map.121 = (f32[16,512]{1,0:T(8,128)}, f32[4,16]{1,0:T(4,128)}, bf16[32,16,512]{2,1,0:T(8,128)(2,1)}, bf16[64,512]{1,0:T(8,128)(2,1)}) custom-call(bf16[32,32,512]{2,1,0:T(8,128)(2,1)S(1)} %all-to-all-done.got, bf16[32,16,512]{2,1,0:T(8,128)(2,1)S(1)} %bitcast.25, bf16[32,16,512]{2,1,0:T(8,128)(2,1)S(1)} %bitcast.26, ...), custom_call_target="tpu_custom_call" | custom-call | bytes 3145728 | tf_op jit(solution)/shard_map/pallas_call | solution.py:201
  (18 shorter events, 0.1 us)
Async XLA Ops:
  0.6 7.8 %copy-start = (bf16[1024,512]{1,0:T(8,128)(2,1)S(1)}, bf16[1024,512]{1,0:T(8,128)(2,1)}, u32[]{:S(2)}) copy-start(bf16[1024,512]{1,0:T(8,128)(2,1)} %tokens.1) | copy-start | bytes 3145732
  0.6 0.9 %copy-start.7 = (bf16[64,512]{1,0:T(8,128)(2,1)S(1)}, bf16[64,512]{1,0:T(8,128)(2,1)}, u32[]{:S(2)}) copy-start(bf16[64,512]{1,0:T(8,128)(2,1)} %rows.1) | copy-start | bytes 196612
  2.4 6.0 %copy-start.1 = (bf16[512,512]{1,0:T(8,128)(2,1)S(1)}, bf16[512,512]{1,0:T(8,128)(2,1)}, u32[]{:S(2)}) copy-start(bf16[512,512]{1,0:T(8,128)(2,1)} %weight.5) | copy-start | bytes 1572868
  2.4 14.5 %all-to-all-start.1 = ((bf16[8,64,512]{2,1,0:T(8,128)(2,1)}), bf16[8,64,512]{2,1,0:T(8,128)(2,1)S(1)}, u32[]{:S(2)}, u32[]{:S(2)}) async-start(bf16[8,64,512]{2,1,0:T(8,128)(2,1)} %shard_map.118), calls=%async_computation.1 | async-start | bytes 1048576 | tf_op jit(solution)/shard_map/all_to_all | solution.py:151
  8.3 0.8 %copy-start.8 = (f32[1,1,16,512]{3,2,1,0:T(8,128)S(1)}, f32[1,1,16,512]{3,2,1,0:T(8,128)}, u32[]{:S(2)}) copy-start(f32[1,1,16,512]{3,2,1,0:T(8,128)} %param.8) | copy-start | bytes 98308
  9.1 1.0 %copy-start.2 = (bf16[1,512,512]{2,1,0:T(8,128)(2,1)S(1)}, bf16[1,512,512]{2,1,0:T(8,128)(2,1)}, u32[]{:S(2)}) copy-start(bf16[1,512,512]{2,1,0:T(8,128)(2,1)} %param.6) | copy-start | bytes 1572868
  10.1 1.0 %copy-start.4 = (bf16[512,512]{1,0:T(8,128)(2,1)S(1)}, bf16[512,512]{1,0:T(8,128)(2,1)}, u32[]{:S(2)}) copy-start(bf16[512,512]{1,0:T(8,128)(2,1)} %stale.1) | copy-start | bytes 1572868
  13.4 1.0 %copy-start.6 = (bf16[32,32,512]{2,1,0:T(8,128)(2,1)}, bf16[32,32,512]{2,1,0:T(8,128)(2,1)S(1)}, u32[]{:S(2)}) copy-start(bf16[32,32,512]{2,1,0:T(8,128)(2,1)S(1)} %get-tuple-element.29) | copy-start | bytes 3145732
  14.4 18.4 %collective-permute-start = (f32[512,512]{1,0:T(8,128)}, f32[512,512]{1,0:T(8,128)}, u32[]{:S(2)}, u32[]{:S(2)}) collective-permute-start(f32[512,512]{1,0:T(8,128)} %get-tuple-element.30), channel_id=1, source_target_pairs={{0,1},{1,0},{2,3},{3,2},{4,5},{5,4},{6,7},{7,6},{8,9},{9,8},{10,11... | collective-permute-start | bytes 3145736 | tf_op jit(solution)/shard_map/ppermute | solution.py:123
  17.0 47.0 %all-to-all-start = ((bf16[32,32,512]{2,1,0:T(8,128)(2,1)}), bf16[32,32,512]{2,1,0:T(8,128)(2,1)S(1)}, u32[]{:S(2)}, u32[]{:S(2)}) async-start(bf16[32,32,512]{2,1,0:T(8,128)(2,1)} %copy-done.6), calls=%async_computation | async-start | bytes 2097152 | tf_op jit(solution)/shard_map/all_to_all | solution.py:173
  35.2 13.3 %collective-permute-start.4 = (bf16[8,64,512]{2,1,0:T(8,128)(2,1)S(1)}, bf16[8,64,512]{2,1,0:T(8,128)(2,1)}, u32[]{:S(2)}, u32[]{:S(2)}) collective-permute-start(bf16[8,64,512]{2,1,0:T(8,128)(2,1)S(1)} %all-to-all-done.1.cot_mine), channel_id=1, source_target_pairs={{0,1},{1,0},{2,3},{3,2},{4,5},{5,4},{6,7},{7,6},{8,9},{9,8},{10,11... | collective-permute-start | bytes 1572872 | tf_op jit(solution)/shard_map/ppermute | solution.py:123
  37.2 15.1 %collective-permute-start.1 = (f32[2,64,512]{2,1,0:T(8,128)}, f32[2,64,512]{2,1,0:T(8,128)}, u32[]{:S(2)}, u32[]{:S(2)}) collective-permute-start(f32[2,64,512]{2,1,0:T(8,128)} %get-tuple-element.35), channel_id=1, source_target_pairs={{0,4},{2,6},{4,0},{6,2},{1,5},{3,7},{5,1},{7,3},{8,12},{10,14},{12... | collective-permute-start | bytes 786440 | tf_op jit(solution)/shard_map/ppermute | solution.py:123
  41.4 13.8 %collective-permute-start.2 = (f32[2,64,512]{2,1,0:T(8,128)}, f32[2,64,512]{2,1,0:T(8,128)}, u32[]{:S(2)}, u32[]{:S(2)}) collective-permute-start(f32[2,64,512]{2,1,0:T(8,128)} %get-tuple-element.36), channel_id=1, source_target_pairs={{0,2},{2,4},{4,6},{6,0},{1,3},{3,5},{5,7},{7,1},{8,10},{10,12},{12... | collective-permute-start | bytes 786440 | tf_op jit(solution)/shard_map/ppermute | solution.py:123
  43.9 11.3 %collective-permute-start.3 = (f32[2,64,512]{2,1,0:T(8,128)}, f32[2,64,512]{2,1,0:T(8,128)}, u32[]{:S(2)}, u32[]{:S(2)}) collective-permute-start(f32[2,64,512]{2,1,0:T(8,128)} %get-tuple-element.37), channel_id=1, source_target_pairs={{0,6},{2,0},{4,2},{6,4},{1,7},{3,1},{5,3},{7,5},{8,14},{10,8},{12,... | collective-permute-start | bytes 786440 | tf_op jit(solution)/shard_map/ppermute | solution.py:123
  55.2 8.8 %copy-start.5 = (bf16[512,512]{1,0:T(8,128)(2,1)S(1)}, bf16[512,512]{1,0:T(8,128)(2,1)}, u32[]{:S(2)}) copy-start(bf16[512,512]{1,0:T(8,128)(2,1)} %stale.1) | copy-start | bytes 1572868
  56.5 7.5 %copy-start.3 = (bf16[1,512,512]{2,1,0:T(8,128)(2,1)S(1)}, bf16[1,512,512]{2,1,0:T(8,128)(2,1)}, u32[]{:S(2)}) copy-start(bf16[1,512,512]{2,1,0:T(8,128)(2,1)} %param.6) | copy-start | bytes 1572868
  56.5 7.5 %collective-permute-start.5 = (f32[64,512]{1,0:T(8,128)S(1)}, f32[64,512]{1,0:T(8,128)S(1)}, u32[]{:S(2)}, u32[]{:S(2)}) collective-permute-start(f32[64,512]{1,0:T(8,128)S(1)} %get-tuple-element.51), channel_id=1, source_target_pairs={{0,8},{8,0},{1,9},{9,1},{2,10},{10,2},{3,11},{11,3},{4,12},{12,4},... | collective-permute-start | bytes 393224 | tf_op jit(solution)/shard_map/ppermute | solution.py:123

commit v5 on v3

--- a/solution.py
+++ b/solution.py
@@ -181,6 +181,7 @@
     )(at, grouped, weight, arrived)
     from_x = [shift(pieces[k - 1], "x", k) for k in (2, 1, 3)]
 
+    kept, cot_mine = lax.optimization_barrier((kept, cot_mine))
     cot_theirs = shift(cot_mine, "core", 1)
     grad_tokens, grad_weight = call(
         grads_kernel,

time: 66.3 us -> 66.3 us (level)
  no operation moved by 1% of the time
where the time goes in v5:
time: 66.3 us; the launch traced here: 65.5 us
  starting transfers between devices  38.4 us (58%)
  Pallas kernels  10.7 us (16%)
  waiting for transfers between devices  8.97 us (14%)
  local copies, waits for them, and re-layouts  4.71 us (7%)
  other arithmetic  2 us (3%)
  between operations  0.79 us (1%)
    ppermute x6, starting transfers between devices, shift(): return lax.ppermute(value, axis, [(i, (i + k) % n) for i in range(n)])  18 us
    all_to_all x1, starting transfers between devices, body(): got = lax.all_to_all(sent, REPLICA, 0, 0)  14.5 us
    all_to_all x1, starting transfers between devices, body(): cot_mine = lax.all_to_all(copies, CHIPS, 0, 0)  5.9 us
    all_to_all x1, waiting for transfers between devices, body(): got = lax.all_to_all(sent, REPLICA, 0, 0)  5.38 us
    unnamed x18, local copies, waits for them, and re-layouts  4.69 us
    pallas_call x1, Pallas kernels, body(): call(grads_kernel, [SMEM, VMEM, VMEM, HBM, HBM], [(tokens.shape, BF16, VM...  3.72 us
    ppermute x6, waiting for transfers between devices, shift(): return lax.ppermute(value, axis, [(i, (i + k) % n) for i in range(n)])  2.96 us
    pallas_call x1, Pallas kernels, body(): call(own_kernel, [SMEM, VMEM, VMEM, VMEM], [((runs, mine, width), F32, VM...  2.41 us
  transfers between devices with their start and end apart: 8, of which 3 were waited for; matrix products, arithmetic and copies ran while one was open for 2% of the time, Pallas kernels for 15%

profile of v5, /device:TPU:72, one launch (start us, length us, event | category | flops | bytes accessed | tf_op | source)
XLA Modules:
  0.0 65.5 jit_solution(11186233537242516305)
XLA Ops:
  0.7 0.9 %copy-done.7 = bf16[64,512]{1,0:T(8,128)(2,1)S(1)} copy-done((bf16[64,512]{1,0:T(8,128)(2,1)S(1)}, bf16[64,512]{1,0:T(8,128)(2,1)}, u32[]{:S(2)}) %copy-start.7) | copy-done | bytes 65560
  1.6 0.8 %shard_map.119 = bf16[8,64,512]{2,1,0:T(8,128)(2,1)} custom-call(bf16[64,512]{1,0:T(8,128)(2,1)S(1)} %copy-done.7), custom_call_target="tpu_custom_call" | custom-call | bytes 1048576 | tf_op jit(solution)/shard_map/pallas_call | solution.py:142
  2.4 5.9 %all-to-all-start.1 = ((bf16[8,64,512]{2,1,0:T(8,128)(2,1)}), bf16[8,64,512]{2,1,0:T(8,128)(2,1)S(1)}, u32[]{:S(2)}, u32[]{:S(2)}) async-start(bf16[8,64,512]{2,1,0:T(8,128)(2,1)} %shard_map.119), calls=%async_computation.1 | async-start | bytes 1048576 | tf_op jit(solution)/shard_map/all_to_all | solution.py:150
  8.3 0.1 pad_add_fusion.at
  8.4 0.7 %copy-done.8 = f32[1,1,16,512]{3,2,1,0:T(8,128)S(1)} copy-done((f32[1,1,16,512]{3,2,1,0:T(8,128)S(1)}, f32[1,1,16,512]{3,2,1,0:T(8,128)}, u32[]{:S(2)}) %copy-start.8) | copy-done | bytes 32792
  9.1 1.0 %copy-done.2 = bf16[1,512,512]{2,1,0:T(8,128)(2,1)S(1)} copy-done((bf16[1,512,512]{2,1,0:T(8,128)(2,1)S(1)}, bf16[1,512,512]{2,1,0:T(8,128)(2,1)}, u32[]{:S(2)}) %copy-start.2) | copy-done | bytes 524312
  10.1 1.0 %copy-done.4 = bf16[512,512]{1,0:T(8,128)(2,1)S(1)} copy-done((bf16[512,512]{1,0:T(8,128)(2,1)S(1)}, bf16[512,512]{1,0:T(8,128)(2,1)}, u32[]{:S(2)}) %copy-start.4) | copy-done | bytes 524312
  11.2 2.2 %shard_map.117 = (bf16[32,32,512]{2,1,0:T(8,128)(2,1)S(1)}, f32[16,512]{1,0:T(8,128)}, f32[512,512]{1,0:T(8,128)}) custom-call(s32[4]{0:T(128)S(1)} %pad_add_fusion.at, bf16[32,16,512]{2,1,0:T(8,128)(2,1)S(1)} %bitcast.26, bf16[512,512]{1,0:T(8,128)(2,1)S(1)} %copy-done.4, f32[16,512]{1,0:T(8,128)S(1)} %bitcast.29, bf16[8,2,64,512]{3,2,1,0:T(8,128)(2,1)S(1)} %bitcast.23, ...), custom_call_target="tpu_custom_call" | custom-call | bytes 3145728 | tf_op jit(solution)/shard_map/pallas_call | solution.py:154
  13.4 1.0 %copy-done.6 = bf16[32,32,512]{2,1,0:T(8,128)(2,1)} copy-done((bf16[32,32,512]{2,1,0:T(8,128)(2,1)}, bf16[32,32,512]{2,1,0:T(8,128)(2,1)S(1)}, u32[]{:S(2)}) %copy-start.6) | copy-done | bytes 1048600
  14.4 1.9 %collective-permute-start = (f32[512,512]{1,0:T(8,128)}, f32[512,512]{1,0:T(8,128)}, u32[]{:S(2)}, u32[]{:S(2)}) collective-permute-start(f32[512,512]{1,0:T(8,128)} %get-tuple-element.32), channel_id=1, source_target_pairs={{0,1},{1,0},{2,3},{3,2},{4,5},{5,4},{6,7},{7,6},{8,9},{9,8},{10,11... | collective-permute-start | bytes 3145736 | tf_op jit(solution)/shard_map/ppermute | solution.py:122
  16.3 0.6 all-to-all-done.1.cot_mine
  17.0 14.5 %all-to-all-start = ((bf16[32,32,512]{2,1,0:T(8,128)(2,1)}), bf16[32,32,512]{2,1,0:T(8,128)(2,1)S(1)}, u32[]{:S(2)}, u32[]{:S(2)}) async-start(bf16[32,32,512]{2,1,0:T(8,128)(2,1)} %copy-done.6), calls=%async_computation | async-start | bytes 2097152 | tf_op jit(solution)/shard_map/all_to_all | solution.py:172
  31.5 2.4 %shard_map.120 = (f32[2,64,512]{2,1,0:T(8,128)S(1)}, f32[2,64,512]{2,1,0:T(8,128)}, f32[2,64,512]{2,1,0:T(8,128)}, f32[2,64,512]{2,1,0:T(8,128)}) custom-call(s32[4]{0:T(128)S(1)} %pad_add_fusion.at, bf16[8,2,64,512]{3,2,1,0:T(8,128)(2,1)S(1)} %bitcast.24, bf16[512,512]{1,0:T(8,128)(2,1)S(1)} %copy-done.1, f32[8,64,512]{2,1,0:T(8,128)} %bitcast.9.arrived), custom_call_target="tpu_custom_call" | custom-call | bytes 2621440 | tf_op jit(solution)/shard_map/pallas_call | solution.py:175
  33.9 1.9 %collective-permute-start.4 = (bf16[8,64,512]{2,1,0:T(8,128)(2,1)S(1)}, bf16[8,64,512]{2,1,0:T(8,128)(2,1)}, u32[]{:S(2)}, u32[]{:S(2)}) collective-permute-start(bf16[8,64,512]{2,1,0:T(8,128)(2,1)S(1)} %all-to-all-done.1.cot_mine), channel_id=1, source_target_pairs={{0,1},{1,0},{2,3},{3,2},{4,5},{5,4},{6,7},{7,6},{8,9},{9,8},{10,11... | collective-permute-start | bytes 1572872 | tf_op jit(solution)/shard_map/ppermute | solution.py:122
  35.8 4.3 %collective-permute-start.1 = (f32[2,64,512]{2,1,0:T(8,128)}, f32[2,64,512]{2,1,0:T(8,128)}, u32[]{:S(2)}, u32[]{:S(2)}) collective-permute-start(f32[2,64,512]{2,1,0:T(8,128)} %get-tuple-element.37), channel_id=1, source_target_pairs={{0,4},{2,6},{4,0},{6,2},{1,5},{3,7},{5,1},{7,3},{8,12},{10,14},{12... | collective-permute-start | bytes 786440 | tf_op jit(solution)/shard_map/ppermute | solution.py:122
  40.1 2.5 %collective-permute-start.2 = (f32[2,64,512]{2,1,0:T(8,128)}, f32[2,64,512]{2,1,0:T(8,128)}, u32[]{:S(2)}, u32[]{:S(2)}) collective-permute-start(f32[2,64,512]{2,1,0:T(8,128)} %get-tuple-element.38), channel_id=1, source_target_pairs={{0,2},{2,4},{4,6},{6,0},{1,3},{3,5},{5,7},{7,1},{8,10},{10,12},{12... | collective-permute-start | bytes 786440 | tf_op jit(solution)/shard_map/ppermute | solution.py:122
  42.6 4.6 %collective-permute-start.3 = (f32[2,64,512]{2,1,0:T(8,128)}, f32[2,64,512]{2,1,0:T(8,128)}, u32[]{:S(2)}, u32[]{:S(2)}) collective-permute-start(f32[2,64,512]{2,1,0:T(8,128)} %get-tuple-element.39), channel_id=1, source_target_pairs={{0,6},{2,0},{4,2},{6,4},{1,7},{3,1},{5,3},{7,5},{8,14},{10,8},{12,... | collective-permute-start | bytes 786440 | tf_op jit(solution)/shard_map/ppermute | solution.py:122
  47.2 3.7 %shard_map.121 = (bf16[1024,512]{1,0:T(8,128)(2,1)}, bf16[512,512]{1,0:T(8,128)(2,1)}) custom-call(s32[4]{0:T(128)S(1)} %pad_add_fusion.at, bf16[1024,512]{1,0:T(8,128)(2,1)S(1)} %copy-done, bf16[512,512]{1,0:T(8,128)(2,1)S(1)} %copy-done.1, bf16[8,64,512]{2,1,0:T(8,128)(2,1)S(1)} %all-to-all-done.1.cot_mine, ...), custom_call_target="tpu_custom_call" | custom-call | bytes 3145728 | tf_op jit(solution)/shard_map/pallas_call | solution.py:186
  50.9 2.9 %collective-permute-done.2 = f32[2,64,512]{2,1,0:T(8,128)} collective-permute-done((f32[2,64,512]{2,1,0:T(8,128)}, f32[2,64,512]{2,1,0:T(8,128)}, u32[]{:S(2)}, u32[]{:S(2)}) %collective-permute-start.2) | collective-permute-done | bytes 262176 | tf_op jit(solution)/shard_map/ppermute | solution.py:122
  53.9 1.3 %add_add_fusion = f32[2,64,512]{2,1,0:T(8,128)S(1)} fusion(f32[2,64,512]{2,1,0:T(8,128)} %collective-permute-done.3, f32[2,64,512]{2,1,0:T(8,128)} %collective-permute-done.2, f32[2,64,512]{2,1,0:T(8,128)S(1)} %get-tuple-element.36, f32[2,64,512]{2,1,0:T(8,128)} %collective-permute-done.1), kind=kLoop, calls=%fused_computation | loop fusion | flops 196608 | bytes 1310720 | tf_op jit(solution)/shard_map/add | solution.py:197
  55.2 2.9 %collective-permute-start.5 = (f32[64,512]{1,0:T(8,128)S(1)}, f32[64,512]{1,0:T(8,128)S(1)}, u32[]{:S(2)}, u32[]{:S(2)}) collective-permute-start(f32[64,512]{1,0:T(8,128)S(1)} %dynamic-slice_bitcast_fusion), channel_id=1, source_target_pairs={{0,8},{8,0},{1,9},{9,1},{2,10},{10,2},{3,11},{11,3},{4,12},{12,4},... | collective-permute-start | bytes 393224 | tf_op jit(solution)/shard_map/ppermute | solution.py:122
  58.0 5.4 %all-to-all-done.got = bf16[32,32,512]{2,1,0:T(8,128)(2,1)S(1)} async-done(((bf16[32,32,512]{2,1,0:T(8,128)(2,1)}), bf16[32,32,512]{2,1,0:T(8,128)(2,1)S(1)}, u32[]{:S(2)}, u32[]{:S(2)}) %all-to-all-start) | async-done | bytes 1048608 | tf_op jit(solution)/shard_map/all_to_all | solution.py:172
  63.4 1.5 %shard_map.118 = (f32[16,512]{1,0:T(8,128)}, f32[4,16]{1,0:T(4,128)}, bf16[32,16,512]{2,1,0:T(8,128)(2,1)}) custom-call(bf16[32,32,512]{2,1,0:T(8,128)(2,1)S(1)} %all-to-all-done.got, bf16[32,16,512]{2,1,0:T(8,128)(2,1)S(1)} %bitcast.27, bf16[32,16,512]{2,1,0:T(8,128)(2,1)S(1)} %bitcast.28, bf16[32,16,512]{2,1,0:T(8,128)(2,1)S(1)} %bitcast.25), custom_call_target="tpu_custom_call" | custom-call | bytes 3145728 | tf_op jit(solution)/shard_map/pallas_call | solution.py:200
  64.9 0.6 fusion
  (19 shorter events, 0.1 us)
Async XLA Ops:
  0.6 7.8 %copy-start = (bf16[1024,512]{1,0:T(8,128)(2,1)S(1)}, bf16[1024,512]{1,0:T(8,128)(2,1)}, u32[]{:S(2)}) copy-start(bf16[1024,512]{1,0:T(8,128)(2,1)} %tokens.1) | copy-start | bytes 3145732
  0.6 0.9 %copy-start.7 = (bf16[64,512]{1,0:T(8,128)(2,1)S(1)}, bf16[64,512]{1,0:T(8,128)(2,1)}, u32[]{:S(2)}) copy-start(bf16[64,512]{1,0:T(8,128)(2,1)} %rows.1) | copy-start | bytes 196612
  2.4 6.0 %copy-start.1 = (bf16[512,512]{1,0:T(8,128)(2,1)S(1)}, bf16[512,512]{1,0:T(8,128)(2,1)}, u32[]{:S(2)}) copy-start(bf16[512,512]{1,0:T(8,128)(2,1)} %weight.5) | copy-start | bytes 1572868
  2.4 14.5 %all-to-all-start.1 = ((bf16[8,64,512]{2,1,0:T(8,128)(2,1)}), bf16[8,64,512]{2,1,0:T(8,128)(2,1)S(1)}, u32[]{:S(2)}, u32[]{:S(2)}) async-start(bf16[8,64,512]{2,1,0:T(8,128)(2,1)} %shard_map.119), calls=%async_computation.1 | async-start | bytes 1048576 | tf_op jit(solution)/shard_map/all_to_all | solution.py:150
  8.3 0.8 %copy-start.8 = (f32[1,1,16,512]{3,2,1,0:T(8,128)S(1)}, f32[1,1,16,512]{3,2,1,0:T(8,128)}, u32[]{:S(2)}) copy-start(f32[1,1,16,512]{3,2,1,0:T(8,128)} %param.8) | copy-start | bytes 98308
  9.1 1.0 %copy-start.2 = (bf16[1,512,512]{2,1,0:T(8,128)(2,1)S(1)}, bf16[1,512,512]{2,1,0:T(8,128)(2,1)}, u32[]{:S(2)}) copy-start(bf16[1,512,512]{2,1,0:T(8,128)(2,1)} %param.6) | copy-start | bytes 1572868
  10.1 1.0 %copy-start.4 = (bf16[512,512]{1,0:T(8,128)(2,1)S(1)}, bf16[512,512]{1,0:T(8,128)(2,1)}, u32[]{:S(2)}) copy-start(bf16[512,512]{1,0:T(8,128)(2,1)} %stale.1) | copy-start | bytes 1572868
  13.4 1.0 %copy-start.6 = (bf16[32,32,512]{2,1,0:T(8,128)(2,1)}, bf16[32,32,512]{2,1,0:T(8,128)(2,1)S(1)}, u32[]{:S(2)}) copy-start(bf16[32,32,512]{2,1,0:T(8,128)(2,1)S(1)} %get-tuple-element.30) | copy-start | bytes 3145732
  14.4 17.1 %collective-permute-start = (f32[512,512]{1,0:T(8,128)}, f32[512,512]{1,0:T(8,128)}, u32[]{:S(2)}, u32[]{:S(2)}) collective-permute-start(f32[512,512]{1,0:T(8,128)} %get-tuple-element.32), channel_id=1, source_target_pairs={{0,1},{1,0},{2,3},{3,2},{4,5},{5,4},{6,7},{7,6},{8,9},{9,8},{10,11... | collective-permute-start | bytes 3145736 | tf_op jit(solution)/shard_map/ppermute | solution.py:122
  17.0 46.4 %all-to-all-start = ((bf16[32,32,512]{2,1,0:T(8,128)(2,1)}), bf16[32,32,512]{2,1,0:T(8,128)(2,1)S(1)}, u32[]{:S(2)}, u32[]{:S(2)}) async-start(bf16[32,32,512]{2,1,0:T(8,128)(2,1)} %copy-done.6), calls=%async_computation | async-start | bytes 2097152 | tf_op jit(solution)/shard_map/all_to_all | solution.py:172
  33.9 13.3 %collective-permute-start.4 = (bf16[8,64,512]{2,1,0:T(8,128)(2,1)S(1)}, bf16[8,64,512]{2,1,0:T(8,128)(2,1)}, u32[]{:S(2)}, u32[]{:S(2)}) collective-permute-start(bf16[8,64,512]{2,1,0:T(8,128)(2,1)S(1)} %all-to-all-done.1.cot_mine), channel_id=1, source_target_pairs={{0,1},{1,0},{2,3},{3,2},{4,5},{5,4},{6,7},{7,6},{8,9},{9,8},{10,11... | collective-permute-start | bytes 1572872 | tf_op jit(solution)/shard_map/ppermute | solution.py:122
  35.8 15.1 %collective-permute-start.1 = (f32[2,64,512]{2,1,0:T(8,128)}, f32[2,64,512]{2,1,0:T(8,128)}, u32[]{:S(2)}, u32[]{:S(2)}) collective-permute-start(f32[2,64,512]{2,1,0:T(8,128)} %get-tuple-element.37), channel_id=1, source_target_pairs={{0,4},{2,6},{4,0},{6,2},{1,5},{3,7},{5,1},{7,3},{8,12},{10,14},{12... | collective-permute-start | bytes 786440 | tf_op jit(solution)/shard_map/ppermute | solution.py:122
  40.1 13.8 %collective-permute-start.2 = (f32[2,64,512]{2,1,0:T(8,128)}, f32[2,64,512]{2,1,0:T(8,128)}, u32[]{:S(2)}, u32[]{:S(2)}) collective-permute-start(f32[2,64,512]{2,1,0:T(8,128)} %get-tuple-element.38), channel_id=1, source_target_pairs={{0,2},{2,4},{4,6},{6,0},{1,3},{3,5},{5,7},{7,1},{8,10},{10,12},{12... | collective-permute-start | bytes 786440 | tf_op jit(solution)/shard_map/ppermute | solution.py:122
  42.6 11.3 %collective-permute-start.3 = (f32[2,64,512]{2,1,0:T(8,128)}, f32[2,64,512]{2,1,0:T(8,128)}, u32[]{:S(2)}, u32[]{:S(2)}) collective-permute-start(f32[2,64,512]{2,1,0:T(8,128)} %get-tuple-element.39), channel_id=1, source_target_pairs={{0,6},{2,0},{4,2},{6,4},{1,7},{3,1},{5,3},{7,5},{8,14},{10,8},{12,... | collective-permute-start | bytes 786440 | tf_op jit(solution)/shard_map/ppermute | solution.py:122
  53.8 9.6 %copy-start.3 = (bf16[1,512,512]{2,1,0:T(8,128)(2,1)S(1)}, bf16[1,512,512]{2,1,0:T(8,128)(2,1)}, u32[]{:S(2)}) copy-start(bf16[1,512,512]{2,1,0:T(8,128)(2,1)} %param.6) | copy-start | bytes 1572868
  53.8 9.6 %copy-start.5 = (bf16[512,512]{1,0:T(8,128)(2,1)S(1)}, bf16[512,512]{1,0:T(8,128)(2,1)}, u32[]{:S(2)}) copy-start(bf16[512,512]{1,0:T(8,128)(2,1)} %stale.1) | copy-start | bytes 1572868
  55.2 9.7 %collective-permute-start.5 = (f32[64,512]{1,0:T(8,128)S(1)}, f32[64,512]{1,0:T(8,128)S(1)}, u32[]{:S(2)}, u32[]{:S(2)}) collective-permute-start(f32[64,512]{1,0:T(8,128)S(1)} %dynamic-slice_bitcast_fusion), channel_id=1, source_target_pairs={{0,8},{8,0},{1,9},{9,1},{2,10},{10,2},{3,11},{11,3},{4,12},{12,4},... | collective-permute-start | bytes 393224 | tf_op jit(solution)/shard_map/ppermute | solution.py:122
